TPU v7x, 32 devices: a whole 2x2x4 slice. The times are simulated.
32 devices in a mesh: row: 4 (over y, x), col: 8 (over z, core).
Axes of the slice: x: 2, y: 2, z: 4, core: 2. Of those that a mesh axis runs over, the one named last changes fastest.
Arguments:
- lower_panel: float32 [8, 10, 5, 2, 256, 256], P('col', None, None, None, 'row'), may hold values from -0.0625 to 0.0625
- diag_inverse: float32 [8, 10, 2, 256, 256], P('col', None, None, 'row'), may hold values from -3 to 3, as said below
- structure: int32 [8, 10, 5], P('col'), may hold values 0 or 1
Outputs:
- sel_panel: float32 [8, 10, 5, 2, 256, 256], P('col', None, None, None, 'row')
- sel_diag: float32 [8, 10, 2, 256, 256], P('col', None, None, 'row')
Inputs may be any that keep to these rules, and one draw needn't show every extreme that they name: Every block diag_inverse[c, s, k] equals its own transpose.
All inputs are finite; a program needn't handle non-finite values. No bound on the sum of `structure` on one device may be relied on, other than what follows from the above.
Results may differ from a plain program's by a relative error of at most 0.0001.
Values sent between devices are 32-bit elements; how exact they have to be, the bound alone decides.
No kernel may reach another device: no remote copies, remote signals or barrier semaphores. Data moves between devices by JAX's collectives and lax.ppermute only.
A program may use at most 128 MiB of HBM per device.

v0:
```python
import functools

import jax
import jax.numpy as jnp
from jax import lax
from jax.experimental import pallas as pl
from jax.experimental.pallas import tpu as pltpu
from jax.sharding import PartitionSpec as P

LEVELS = 6
HALVES = 2
VMEM_BYTES = 18 * 2**20
PACK_BYTES = 58 * 2**20
F32 = jnp.float32
BF16 = jnp.bfloat16
ANY = pl.BlockSpec(memory_space=pl.ANY)
VMEM = pl.BlockSpec(memory_space=pltpu.VMEM)
SMEM = pl.BlockSpec(memory_space=pltpu.SMEM)


def turned(mask, rows):
    if rows < 4:
        return mask
    return (mask & ~3) | ((mask & 1) << 1) | ((mask >> 1) & 1)


def col_swap(value):
    count = lax.axis_size("col")
    return lax.ppermute(value, "col", [(source, source ^ 1) for source in range(count)])


def row_swap(value, mask):
    rows, columns = lax.axis_size("row"), lax.axis_size("col")
    pairs = []
    for row in range(rows):
        for col in range(columns):
            other = row ^ (turned(mask, rows) if col % 2 else mask)
            pairs.append((row * columns + col, other * columns + col))
    return lax.ppermute(value, ("row", "col"), pairs)


def rows_of(scalars, mask, chunk):
    away = mask & ~3
    if mask & 1:
        away = away | scalars[3]
    if mask & 2:
        away = away | scalars[4]
    return pl.multiple_of((scalars[0] ^ away) * chunk, chunk)


def split(value):
    high = value.astype(BF16)
    return high, (value - high.astype(F32)).astype(BF16)


WIDE = 3


def store_left(ref, rows, first, value):
    high, low = split(value)
    size = value.shape[1]
    for at, part in enumerate((high, high, low)):
        ref[rows, pl.ds(first + at * size, size)] = part


def store_right(ref, first, value):
    high, low = split(value)
    size = value.shape[0]
    for at, part in enumerate((high, low, high)):
        ref[pl.ds(first + at * size, size)] = part


def times(left, right):
    return jnp.dot(left, right, preferred_element_type=F32)


def complex_sum(product, half):
    count = product.shape[0] // 2
    by_real, by_imag = product[:count], product[count:]
    return jnp.concatenate(
        [by_real[:, :half] - by_imag[:, half:], by_real[:, half:] + by_imag[:, :half]], axis=1
    )


def run_kernel(kernel, outs, ins, scratch, flops, aliases=None, limit=VMEM_BYTES):
    moved = sum(value.size for value, _ in ins)
    return pl.pallas_call(
        kernel,
        out_shape=[jax.ShapeDtypeStruct(shape, dtype) for shape, dtype, _ in outs],
        in_specs=[spec for _, spec in ins],
        out_specs=[spec for _, _, spec in outs],
        scratch_shapes=scratch,
        input_output_aliases=aliases or {},
        compiler_params=pltpu.CompilerParams(vmem_limit_bytes=limit),
        cost_estimate=pl.CostEstimate(flops=flops // 64, bytes_accessed=moved // 64, transcendentals=0),
    )(*[value for value, _ in ins])


class Loads:
    def __init__(self, sources, buffers, sems):
        self.buffers = buffers
        self.copies = [
            pltpu.make_async_copy(source, buffer, sems.at[at])
            for at, (source, buffer) in enumerate(zip(sources, buffers))
        ]
        for copy in self.copies:
            copy.start()

    def get(self, at):
        if self.copies[at] is not None:
            self.copies[at].wait()
            self.copies[at] = None
        return self.buffers[at]


def both_parts(mask, array, base=0):
    return [(mask, 0, array, 2 * base, 2), (mask, 1, array, 2 * base + 1, 2)]


def pack_kernel(spans, plan, n_outs, chunk, *refs):
    scalars, present, panel_ref, diag_ref = refs[:4]
    outs = refs[4 : 4 + n_outs]
    panel_bufs = refs[4 + n_outs : -2]
    diag_buf, sems = refs[-2:]
    sources, buffers = [], []
    for (first, nodes, depth), buffer in zip(spans, panel_bufs):
        sources.append(panel_ref.at[0, pl.ds(first, nodes), pl.ds(0, depth)])
        buffers.append(buffer)
    if any(block == 0 for blocks in plan for _, _, block in blocks):
        sources.append(diag_ref.at[0])
        buffers.append(diag_buf)
    loads = Loads(sources, buffers, sems)
    where = {first: at for at, (first, _, _) in enumerate(spans)}
    for out, blocks in zip(outs, plan):
        for at, (first, node_of, block) in enumerate(blocks):
            node = node_of(scalars[2])
            if block == 0:
                value = loads.get(len(spans))[first + node]
            else:
                scale = present[first + node, block - 1].astype(F32)
                value = loads.get(where[first])[node, block - 1] * scale
            out[pl.ds(2 * at, 2)] = value


def pack(plan, spans, scalars, present, lower_panel, diag_inverse, limit):
    chunk, width = lower_panel.shape[-2:]
    outs = [((2 * len(blocks), chunk, width), F32, VMEM) for blocks in plan]
    scratch = [pltpu.VMEM((nodes, depth, 2, chunk, width), F32) for _, nodes, depth in spans]
    scratch += [pltpu.VMEM(diag_inverse.shape[1:], F32), pltpu.SemaphoreType.DMA((len(spans) + 1,))]
    kernel = functools.partial(pack_kernel, spans, plan, len(outs), chunk)
    ins = [(scalars, SMEM), (present, SMEM), (lower_panel, ANY), (diag_inverse, ANY)]
    return run_kernel(kernel, outs, ins, scratch, 0, limit=limit)


def pack_last_kernel(first, nodes, depth, steps, cols, *refs):
    scalars, present, panel_ref = refs[:3]
    outs = refs[3 : 3 + len(steps) * HALVES]
    buffer, sem = refs[-2:]
    copy = pltpu.make_async_copy(panel_ref.at[0, pl.ds(first, nodes), pl.ds(0, depth)], buffer, sem)
    copy.start()
    copy.wait()
    for at, (step, group) in enumerate(steps):
        node = (scalars[2] // group) ^ step
        for block in range(depth):
            value = buffer[node, block] * present[first + node, block].astype(F32)
            for half in range(HALVES):
                outs[half * len(steps) + at][pl.ds(2 * block, 2)] = value[
                    :, :, half * cols : (half + 1) * cols
                ]


def pack_last(first, nodes, depth, steps, cols, scalars, present, lower_panel):
    chunk, width = lower_panel.shape[-2:]
    outs = [((2 * depth, chunk, cols), F32, VMEM)] * (len(steps) * HALVES)
    scratch = [pltpu.VMEM((nodes, depth, 2, chunk, width), F32), pltpu.SemaphoreType.DMA]
    kernel = functools.partial(pack_last_kernel, first, nodes, depth, steps, cols)
    ins = [(scalars, SMEM), (present, SMEM), (lower_panel, ANY)]
    return run_kernel(kernel, outs, ins, scratch, 0)


def prep_kernel(levels, table, rows_count, chunk, width, n_arrays, *refs):
    scalars, present = refs[:2]
    arrays = refs[2 : 2 + n_arrays]
    outs = list(refs[2 + n_arrays :])
    odd = scalars[1] == 1
    for depth, swapped, first, slot in levels:
        if depth:
            whole, forward = outs.pop(0), outs.pop(0)
        else:
            whole = None
        backward = outs.pop(0)
        for block in range(depth + 1):
            for mask, part, position, base, stride in table:
                plane = base + stride * (first + block)
                start = rows_of(scalars, mask, chunk)
                if swapped is None:
                    value = arrays[position][plane]
                else:
                    half = n_arrays // 2
                    from_odd = arrays[position + (0 if swapped else half)]
                    from_even = arrays[position + (half if swapped else 0)]
                    value = jnp.where(odd, from_odd[plane], from_even[plane])
                    away = turned(mask, rows_count) if swapped else mask
                    start = pl.multiple_of((scalars[0] ^ away) * chunk, chunk)
                if block == 0:
                    rows = pl.ds(pl.multiple_of(part * width + start, chunk), chunk)
                    store_left(backward, rows, WIDE * depth * width, value)
                else:
                    if slot is not None:
                        at = slot[0] + scalars[2] // slot[1]
                        value = value * present[at, block - 1].astype(F32)
                    rows = pl.ds(pl.multiple_of((depth - block) * width + start, chunk), chunk)
                    whole[rows, pl.ds(part * width, width)] = value
        for level in range(depth):
            for part in range(2):
                value = whole[pl.ds(level * width, width), pl.ds(part * width, width)]
                store_left(forward, pl.ds((2 * level + part) * width, width), 0, value)
                rows = pl.ds(part * width, width)
                store_left(backward, rows, WIDE * level * width, -value.T)


def prep(levels, pieces, scalars, present, rows, chunk, width, others=()):
    arrays, table = [], []
    for mask, part, array, base, stride in pieces:
        position = next((at for at, value in enumerate(arrays) if value is array), None)
        if position is None:
            position = len(arrays)
            arrays.append(array)
        table.append((mask, part, position, base, stride))
    arrays = arrays + list(others)
    outs = []
    for depth, _, _, _ in levels:
        if depth:
            outs.append(((depth * width, 2 * width), F32, VMEM))
            outs.append(((2 * depth * width, WIDE * width), BF16, VMEM))
        outs.append(((2 * width, WIDE * (depth + 1) * width), BF16, VMEM))
    kernel = functools.partial(prep_kernel, levels, table, rows, chunk, width, len(arrays))
    ins = [(scalars, SMEM), (present, SMEM)] + [(value, VMEM) for value in arrays]
    made = list(run_kernel(kernel, outs, ins, [], 0))
    result = {}
    for depth, _, _, _ in levels:
        if depth:
            result[depth], made = tuple(made[:3]), made[3:]
        else:
            result[depth], made = (None, None, made[0]), made[1:]
    return result


def substitute(depth, width, cols, get, sums, right, emit):
    def rows(first, count=1):
        return pl.ds(first * width, count * width)

    for level in range(depth - 1, 0, -1):
        store_right(right, WIDE * level * width, sums[rows(level)])
        forward = get("forward", level)
        for block in range(level - 1, -1, -1):
            product = times(forward[rows(2 * block, 2)], right[rows(WIDE * level, WIDE)])
            sums[rows(block)] -= complex_sum(product, cols)
    store_right(right, 0, sums[rows(0)])
    for level in range(depth):
        product = times(get("backward", level)[...], right[rows(0, WIDE * (level + 1))])
        solved = complex_sum(product, cols)
        store_right(right, WIDE * level * width, solved)
        emit(level, solved)


def solve_kernel(depths, chunk, width, steps, order, masked, *refs):
    refs = list(refs)
    scalars = refs.pop(0)
    sources = [refs.pop(0) for _ in order]
    outs = {depth: [(refs.pop(0), refs.pop(0)) for _ in steps] for depth in depths}
    sums_ref, right_ref, solved_ref = refs

    def get(kind, level):
        return sources[order.index((kind, level))]

    for depth in depths:
        sums = sums_ref.at[pl.ds(0, depth * width)]
        right = right_ref.at[pl.ds(0, WIDE * depth * width)]
        sums[...] = get("whole", depth)[...]

        def send(block, value, sign):
            solved_ref[...] = value
            for (out, correction), step in zip(outs[depth], steps):
                start = rows_of(scalars, step, chunk)
                piece = solved_ref[pl.ds(start, chunk)] * sign
                if depth in masked:
                    piece = jnp.where(scalars[5 + depth] == 1, piece, 0.0)
                for part in range(2):
                    plane = piece[:, part * width : (part + 1) * width]
                    if block == 0:
                        correction[part] = plane
                    else:
                        out[block - 1, part] = plane

        substitute(
            depth, width, width, get, sums, right,
            lambda level, solved: send(depth - level, solved, -1.0),
        )
        product = times(get("backward", depth)[:, : WIDE * depth * width], right[...])
        send(0, complex_sum(product, width), 1.0)


def operands(made, names):
    index = {"whole": 0, "forward": 1, "backward": 2}
    return [made[level][index[kind]] for kind, level in names]


def solve(depths, made, scalars, steps, chunk, width, masked):
    top = depths[0]
    order = [("whole", top)]
    for level in range(top - 1, 0, -1):
        order.append(("forward", level))
    for level in range(top + 1):
        order.append(("backward", level))
    order += [("whole", depth) for depth in depths[1:]]
    sources = operands(made, order)
    outs = []
    for depth in depths:
        for _ in steps:
            outs.append(((depth, 2, chunk, width), F32, VMEM))
            outs.append(((2, chunk, width), F32, VMEM))
    scratch = [
        pltpu.VMEM((top * width, 2 * width), F32),
        pltpu.VMEM((WIDE * top * width, 2 * width), BF16),
        pltpu.VMEM((width, 2 * width), F32),
    ]
    kernel = functools.partial(solve_kernel, depths, chunk, width, steps, order, masked)
    flops = sum(24 * (depth * depth + depth) * width**3 for depth in depths)
    ins = [(scalars, SMEM)] + [(value, VMEM) for value in sources]
    got = list(run_kernel(kernel, outs, ins, scratch, flops))
    result = {}
    for depth in depths:
        result[depth] = [(got.pop(0), got.pop(0)) for _ in steps]
    return result


def last_kernel(depth, chunk, width, cols, steps, table, n_arrays, order, n_done, *refs):
    refs = list(refs)
    scalars = refs.pop(0)
    arrays = [refs.pop(0) for _ in range(n_arrays)]
    sources = [refs.pop(0) for _ in order]
    lefts = [(refs.pop(0), refs.pop(0)) for _ in range(n_done)]
    outs = [refs.pop(0) for _ in steps]
    left, right = refs.pop(0), refs.pop(0)
    sums, solved_ref, total = refs

    def get(kind, level):
        return sources[order.index((kind, level))]

    for mask, part, position, base, stride in table:
        start = rows_of(scalars, mask, chunk)
        for block in range(depth):
            row = pl.multiple_of((depth - 1 - block) * width + start, chunk)
            sums[pl.ds(row, chunk), pl.ds(part * cols, cols)] = arrays[position][base + stride * block]
    for level in range(depth):
        for part in range(2):
            value = sums[pl.ds(level * width, width), pl.ds(part * cols, cols)]
            store_left(left, pl.ds(part * cols, cols), WIDE * level * width, value.T)

    def emit(level, value):
        solved_ref[...] = value
        for out, step in zip(outs, steps):
            start = rows_of(scalars, step, chunk)
            piece = -solved_ref[pl.ds(start, chunk)]
            out[depth - 1 - level, 0] = piece[:, :cols]
            out[depth - 1 - level, 1] = piece[:, cols:]

    substitute(depth, width, cols, get, sums, right, emit)


    if n_done + 1 < HALVES:
        return
    lefts.append((left, right))
    for row in range(HALVES):
        for col in range(HALVES):
            block = -complex_sum(times(lefts[row][0][...], lefts[col][1][...]), cols)
            for part in range(2):
                total[col, part, pl.ds(row * cols, cols)] = block[:, part * cols : (part + 1) * cols]
    for out, step in zip(outs, steps):
        start = rows_of(scalars, step, chunk)
        for col in range(HALVES):
            for part in range(2):
                out[depth + col, part] = total[col, part, pl.ds(start, chunk)]


def solve_last(depth, made, pieces, scalars, steps, chunk, width, cols, lefts):
    arrays, table = [], []
    for mask, part, array, base, stride in pieces:
        position = next((at for at, value in enumerate(arrays) if value is array), None)
        if position is None:
            position = len(arrays)
            arrays.append(array)
        table.append((mask, part, position, base, stride))
    order = []
    for level in range(depth - 1, 0, -1):
        order.append(("forward", level))
    for level in range(depth):
        order.append(("backward", level))
    done = len(lefts) + 1 == HALVES
    sources = operands(made, order) + ([value for left in lefts for value in left] if done else [])
    blocks = depth + (HALVES if done else 0)
    outs = [((blocks, 2, chunk, cols), F32, VMEM)] * len(steps)
    outs.append(((2 * cols, WIDE * depth * width), BF16, VMEM))
    outs.append(((WIDE * depth * width, 2 * cols), BF16, VMEM))
    scratch = [
        pltpu.VMEM((depth * width, 2 * cols), F32),
        pltpu.VMEM((width, 2 * cols), F32),
        pltpu.VMEM((HALVES, 2, width, cols), F32),
    ]
    kernel = functools.partial(
        last_kernel, depth, chunk, width, cols, steps, table, len(arrays), order,
        len(lefts) if done else 0,
    )
    flops = 24 * depth * depth * width * width * cols
    ins = [(scalars, SMEM)] + [(value, VMEM) for value in arrays]
    ins += [(value, VMEM) for value in sources]
    got = run_kernel(kernel, outs, ins, scratch, flops)
    return got[: len(steps)], got[len(steps) :]


def begin_kernel(plan, zeros, *refs):
    scalars = refs[0]
    pieces = refs[1 : 1 + len(plan)]
    out, zero_ref, sem = refs[1 + len(plan) :]
    zero_ref[...] = jnp.zeros_like(zero_ref)
    copies = []
    for slot, depth, count in zeros:
        copies.append((zero_ref.at[pl.ds(0, count)], out.at[0, slot, pl.ds(depth, count)]))
    for piece, (first, group, step, depth) in zip(pieces, plan):
        slot = first + ((scalars[2] // group) ^ step)
        copies.append((piece, out.at[0, slot, pl.ds(0, depth)]))
    copies = [
        pltpu.make_async_copy(source, target, sem.at[at])
        for at, (source, target) in enumerate(copies)
    ]
    for copy in copies:
        copy.start()
    for copy in copies:
        copy.wait()


def place_kernel(plan, depth, cols, half, diag_plan, shared, *refs):
    refs = list(refs)
    scalars = refs.pop(0)
    pieces = [refs.pop(0) for _ in plan]
    refs.pop(0)
    last_half = half + 1 == HALVES
    own = refs.pop(0) if last_half else None
    corrections = [refs.pop(0) for _ in diag_plan] if last_half else []
    out = refs.pop(0)
    diag = refs.pop(0) if last_half else None
    (sem,) = refs
    copies = []
    slots = [first + ((scalars[2] // group) ^ step) for first, group, step in plan]
    for at, (piece, slot) in enumerate(zip(pieces, slots)):
        target = out.at[0, slot, :, :, :, pl.ds(half * cols, cols)]
        copies.append(pltpu.make_async_copy(piece.at[pl.ds(0, depth)], target, sem.at[at]))
    for copy in copies:
        copy.start()
    if last_half:
        for slot in range(diag.shape[1]):
            value = own[0, slot]
            if slot in shared:
                value = jnp.where(scalars[5 + shared[slot]] == 1, value, 0.0)
            diag[0, slot] = value
        for correction, (first, group, step) in zip(corrections, diag_plan):
            slot = first + ((scalars[2] // group) ^ step)
            diag[0, slot] = diag[0, slot] - correction[...]
        for piece, slot in zip(pieces, slots):
            for col in range(HALVES):
                lanes = slice(col * cols, (col + 1) * cols)
                diag[0, slot, :, :, lanes] = diag[0, slot, :, :, lanes] - piece[depth + col]
    for copy in copies:
        copy.wait()


def body(lower_panel, diag_inverse, structure):
    columns = lax.axis_size("col")
    rows = lax.axis_size("row")
    position = lax.axis_index("col")
    place = lax.axis_index("row")
    slots, anc_count, _, chunk, width = lower_panel.shape[1:]
    per_col = [max(1, 2**depth // columns) for depth in range(LEVELS)]
    offsets = [sum(per_col[:depth]) for depth in range(LEVELS)]
    last = LEVELS - 1
    cols = width // HALVES
    groups = [rows // nodes for nodes in per_col]
    steps = [[step * groups[depth] for step in range(per_col[depth])] for depth in range(LEVELS)]
    shared = [depth for depth in range(LEVELS) if 2**depth < columns]
    middle = [depth for depth in range(LEVELS - 1) if 2**depth >= columns]
    active = [position % max(1, columns // 2**depth) == 0 for depth in range(LEVELS)]
    odd = position % 2 == 1
    scalars = [place, odd, jnp.where(odd, turned(place, rows), place)]
    scalars += [jnp.where(odd, turned(mask, rows), mask) for mask in (1, 2)]
    scalars = jnp.stack([jnp.asarray(value, jnp.int32) for value in scalars + active])
    present = structure[0]

    upper = shared[:-1]
    starts = [sum(1 + depth for depth in upper[:at]) for at in range(len(upper))]

    def level_blocks(depth, step=0):
        group = groups[depth]
        return [
            (offsets[depth], lambda at, group=group, step=step: (at // group) ^ step, block)
            for block in range(depth + 1)
        ]

    def packs(plan, depths, limit):
        spans = [(offsets[depth], per_col[depth], depth) for depth in depths if depth]
        return list(pack(plan, spans, scalars, present, lower_panel, diag_inverse, limit))

    plan = [sum([level_blocks(depth) for depth in upper], []), level_blocks(shared[-1])]
    near_rows, far_rows, bases = [], [], {}
    virtual = jnp.where(odd, turned(place, rows), place)
    for depth in middle:
        bases[depth] = sum(1 + held for held in bases)
        group, first = groups[depth], offsets[depth]
        for kept, step in ((near_rows, 0), (far_rows, 0 if group > 2 else 1)):
            slot = first + ((virtual // group) ^ step)
            diag = lax.dynamic_index_in_dim(diag_inverse[0], slot, 0, keepdims=False)
            panels = lax.dynamic_index_in_dim(lower_panel[0], slot, 0, keepdims=False)[:depth]
            kept += [diag, panels.reshape(2 * depth, chunk, width)]
    packed = packs(plan, shared, PACK_BYTES)
    upper_pack, own_pack = packed[:2]

    stride = columns // 2
    while stride >= 4:
        held = [at for at, depth in enumerate(upper) if columns // 2**depth >= 2 * stride]
        count = 2 * (starts[held[-1]] + 1 + upper[held[-1]])
        pairs = [(source, source + stride) for source in range(0, columns, 2 * stride)]
        if stride == columns // 2 and count == 2:
            travelling = diag_inverse[0, 0]
        else:
            travelling = upper_pack[:count]
        arrived = lax.ppermute(travelling, "col", pairs)
        fresh = position % (2 * stride) == stride
        upper_pack = jnp.concatenate(
            [jnp.where(fresh, arrived, upper_pack[:count]), upper_pack[count:]], axis=0
        )
        stride //= 2
    from_one = lax.ppermute(
        upper_pack, "col", [(source, source + 1) for source in range(0, columns, 4)]
    )
    from_three = lax.ppermute(
        upper_pack, "col", [(source, source + 3) for source in range(0, columns, 4)]
    )
    if middle:
        near_pack = jnp.concatenate(near_rows, axis=0)
        far_pack = jnp.concatenate(far_rows, axis=0)
        near_got = row_swap(near_pack, 1)
        far_got = row_swap(far_pack, 2)
        from_one, from_three, near_got, far_got = lax.optimization_barrier(
            (from_one, from_three, near_got, far_got)
        )
    upper_got = jnp.where(position % 4 == 1, from_one, from_three)
    planes = max(own_pack.shape[0], upper_got.shape[0])

    def fill(value):
        return jnp.pad(value, ((0, planes - value.shape[0]), (0, 0), (0, 0)))

    own = jnp.where(odd, fill(upper_got), fill(own_pack))

    near = row_swap(own, 1)
    far = row_swap(own, 2)

    def halves(value):
        return value.reshape(value.shape[0] // 2, 2, chunk, width)

    near_sends, far_sends = [halves(far)[:, 0]], [halves(near)[:, 1]]
    homes = {}
    near_size = far_size = planes // 2
    for depth in middle:
        first, count = 2 * bases[depth], 2 * (depth + 1)
        homes[depth] = (near_size, far_size)
        if groups[depth] > 2:
            near_sends.append(halves(far_got[first : first + count])[:, 0])
            far_sends.append(halves(near_got[first : first + count])[:, 1])
            near_size += depth + 1
            far_size += depth + 1
        else:
            near_sends.append(far_got[first : first + count])
            near_size += count
    near_sends = jnp.concatenate(near_sends, axis=0)
    far_sends = jnp.concatenate(far_sends, axis=0)
    nodes, group = per_col[last], groups[last]
    last_packs = pack_last(
        offsets[last], nodes, last, [(step, group) for step in range(nodes)], cols,
        scalars, present, lower_panel,
    )
    near_sends, far_sends, last_packs = lax.optimization_barrier(
        (near_sends, far_sends, last_packs)
    )
    near_more = row_swap(near_sends, 1)
    far_more = row_swap(far_sends, 2)
    near_more, far_more, last_packs = lax.optimization_barrier((near_more, far_more, last_packs))

    blocks = planes // 2
    mine = jnp.concatenate([own, near, far, near_more[:blocks], far_more[:blocks]], axis=0)
    theirs = col_swap(mine)
    shared_pieces = (
        both_parts(0, mine)
        + both_parts(1, mine, blocks)
        + both_parts(2, mine, 2 * blocks)
        + [(3, 0, mine, 6 * blocks, 1), (3, 1, mine, 7 * blocks, 1)]
    )

    made = {}
    for depth in middle:
        base = bases[depth]
        near_home, far_home = homes[depth]
        pieces = both_parts(0, near_pack, base) + both_parts(1, near_got, base)
        pieces += both_parts(2, far_got, base)
        if groups[depth] > 2:
            pieces += [(3, 0, near_more, near_home, 1), (3, 1, far_more, far_home, 1)]
        else:
            pieces += [(3, 0, near_more, near_home, 2), (3, 1, near_more, near_home + 1, 2)]
        level = (depth, None, 0, (offsets[depth], groups[depth]))
        made.update(prep([level], pieces, scalars, present, rows, chunk, width))
    levels = [(depth, True, starts[at], None) for at, depth in enumerate(upper)]
    levels.append((shared[-1], False, 0, None))
    made.update(
        prep(levels, shared_pieces, scalars, present, rows, chunk, width, others=[theirs])
    )
    last_pieces = []
    for half in range(HALVES):
        sent = last_packs[half * nodes : (half + 1) * nodes]
        if half:
            sent, made = lax.optimization_barrier((sent, made))
        pieces = []
        for step, value in zip(steps[last], sent):
            arrived = row_swap(value, step) if step else value
            if group == 1:
                pieces.append((step, arrived))
                continue
            listed = [(step, arrived)]
            mask = 1
            while mask < group:
                listed += [(mask | at, row_swap(held, mask)) for at, held in listed]
                mask *= 2
            pieces += listed
        last_pieces.append(pieces)

    single = [depth for depth in range(last - 1, 0, -1) if per_col[depth] == 1]
    solved = {}
    for depth in range(1, last):
        if per_col[depth] > 1:
            solved.update(solve([depth], made, scalars, steps[depth], chunk, width, ()))
    second = [value for _, value in last_pieces[-1][:2]]
    solved, second, later = lax.optimization_barrier((solved, second, scalars))
    last_pieces[-1][:2] = [
        (at, value) for (at, _), value in zip(last_pieces[-1][:2], second)
    ]
    lefts, backs = [], []
    for half in range(HALVES):
        outward, left = solve_last(
            last, made, sum([both_parts(at, held) for at, held in last_pieces[half]], []),
            later, steps[last], chunk, width, cols, lefts
        )
        lefts.append(left)
        if half + 1 == HALVES:
            outward, later = lax.optimization_barrier((outward, scalars))
        backs.append(
            [row_swap(piece, step) if step else piece for piece, step in zip(outward, steps[last])]
        )
    solved.update(solve(single, made, later, [0], chunk, width, tuple(shared)))

    begin_plan, begin_pieces, diag_plan, diag_pieces = [], [], [], []
    for depth in range(1, last):
        for step, (piece, correction) in enumerate(solved[depth]):
            if step:
                both = jnp.concatenate([piece, correction[None]], axis=0)
                both = row_swap(both, steps[depth][step])
                piece, correction = both[:depth], both[depth]
            begin_plan.append((offsets[depth], groups[depth], step, depth))
            begin_pieces.append(piece)
            diag_plan.append((offsets[depth], groups[depth], step))
            diag_pieces.append(correction)
    zeros = [
        (offsets[depth] + node, depth, anc_count - depth)
        for depth in range(LEVELS)
        for node in range(per_col[depth])
        if depth < anc_count
    ]
    panel_shape = lower_panel.shape
    (sel_panel,) = run_kernel(
        functools.partial(begin_kernel, begin_plan, zeros),
        [(panel_shape, F32, ANY)],
        [(scalars, SMEM)] + [(piece, VMEM) for piece in begin_pieces],
        [
            pltpu.VMEM((anc_count, 2, chunk, width), F32),
            pltpu.SemaphoreType.DMA((len(zeros) + len(begin_plan),)),
        ],
        0,
    )
    last_plan = [(offsets[last], group, step) for step in range(nodes)]
    masked = {offsets[depth]: depth for depth in shared}
    for half, back in enumerate(backs):
        ins = [(scalars, SMEM)] + [(piece, VMEM) for piece in back] + [(sel_panel, ANY)]
        outs = [(panel_shape, F32, ANY)]
        if half + 1 == HALVES:
            ins += [(diag_inverse, VMEM)] + [(piece, VMEM) for piece in diag_pieces]
            outs.append((diag_inverse.shape, F32, VMEM))
        made_now = run_kernel(
            functools.partial(place_kernel, last_plan, last, cols, half, diag_plan, masked),
            outs,
            ins,
            [pltpu.SemaphoreType.DMA((nodes,))],
            0,
            aliases={1 + nodes: 0},
        )
        sel_panel = made_now[0]
    return (sel_panel, made_now[1])


def solution(mesh):
    in_specs = (
        P("col", None, None, None, "row", None),
        P("col", None, None, "row", None),
        P("col", None, None),
    )
    out_specs = (P("col", None, None, None, "row", None), P("col", None, None, "row", None))
    return jax.shard_map(body, mesh=mesh, in_specs=in_specs, out_specs=out_specs, check_vma=False)
```

profile of v0, /device:TPU:0, one launch (start us, length us, event | category | flops | bytes accessed | tf_op | source)
XLA Modules:
  0.0 153.7 jit_solution(9505689736244309426)
XLA Ops:
  3.0 1.8 %dynamic-slice_bitcast_fusion = (f32[2,64,256]{2,1,0:T(8,128)S(1)}, f32[2,64,256]{2,1,0:T(8,128)S(1)}, f32[2,64,256]{2,1,0:T(8,128)S(1)}, f32[2,64,256]{2,1,0:T(8,128)}) fusion(f32[1,10,2,64,256]{4,3,2,1,0:T(8,128)} %refs_6_.1, s32[]{:T(128)S(6)} %select_n.99, s32[]{:T(128)S(6)} %select_n.98, s32[]{:T(128)S(6)} %select_n.96), kind=kLoop, calls=%fused_computation.16 | loop fusion | bytes 1048588 | tf_op jit(solution)/shard_map/jit(dynamic_index_in_dim)/squeeze | solution.py:521
  4.8 1.3 fusion.1
  6.1 3.0 %collective-permute-start.4 = (f32[18,64,256]{2,1,0:T(8,128)}, f32[18,64,256]{2,1,0:T(8,128)S(1)}, u32[]{:S(2)}, u32[]{:S(2)}) collective-permute-start(f32[18,64,256]{2,1,0:T(8,128)} %get-tuple-element.202), channel_id=1, source_target_pairs={{0,16},{1,9},{2,18},{3,11},{4,20},{5,13},{6,22},{7,15},{8,24},{9,1... | collective-permute-start | bytes 3538952 | tf_op jit(solution)/shard_map/ppermute | solution.py:39
  9.1 1.5 collective-permute-start.3
  10.5 5.1 %collective-permute-start = (f32[2,64,256]{2,1,0:T(8,128)}, f32[2,64,256]{2,1,0:T(8,128)}, u32[]{:S(2)}, u32[]{:S(2)}) collective-permute-start(f32[2,64,256]{2,1,0:T(8,128)} %get-tuple-element.201), channel_id=1, source_target_pairs={{0,4},{8,12},{16,20},{24,28}} | collective-permute-start | bytes 393224 | tf_op jit(solution)/shard_map/ppermute | solution.py:536
  17.0 3.2 %shard_map.50 = (f32[6,64,256]{2,1,0:T(8,128)}, f32[6,64,256]{2,1,0:T(8,128)}) custom-call(s32[11]{0:T(128)} %stack.54.refs_0_, s32[10,5]{1,0:T(8,128)} %bitcast.44, f32[1,10,5,2,64,256]{5,4,3,2,1,0:T(8,128)} %refs_2_.3, f32[1,10,2,64,256]{4,3,2,1,0:T(8,128)} %refs_6_.1), custom_call_target="tpu_custom_call" | custom-call | bytes 30720 | tf_op jit(solution)/shard_map/pallas_call | solution.py:87
  23.0 2.0 %collective-permute-start.2 = (f32[6,64,256]{2,1,0:T(8,128)}, f32[6,64,256]{2,1,0:T(8,128)}, u32[]{:S(2)}, u32[]{:S(2)}) collective-permute-start(f32[6,64,256]{2,1,0:T(8,128)} %pad_maximum_fusion.5), channel_id=1, source_target_pairs={{0,3},{4,7},{8,11},{12,15},{16,19},{20,23},{24,27},{28,31}} | collective-permute-start | bytes 1179656 | tf_op jit(solution)/shard_map/ppermute | solution.py:545
  25.0 2.1 %collective-permute-start.1 = (f32[6,64,256]{2,1,0:T(8,128)}, f32[6,64,256]{2,1,0:T(8,128)}, u32[]{:S(2)}, u32[]{:S(2)}) collective-permute-start(f32[6,64,256]{2,1,0:T(8,128)} %pad_maximum_fusion.5), channel_id=1, source_target_pairs={{0,1},{4,5},{8,9},{12,13},{16,17},{20,21},{24,25},{28,29}} | collective-permute-start | bytes 1179656 | tf_op jit(solution)/shard_map/ppermute | solution.py:542
  27.1 2.9 %copy-done = f32[1,10,5,2,64,256]{5,4,3,2,1,0:T(8,128)S(1)} copy-done((f32[1,10,5,2,64,256]{5,4,3,2,1,0:T(8,128)S(1)}, f32[1,10,5,2,64,256]{5,4,3,2,1,0:T(8,128)}, u32[]{:S(2)}) %copy-start) | copy-done | bytes 6553624
  31.0 4.8 %collective-permute-done.4.refs_4_ = f32[18,64,256]{2,1,0:T(8,128)S(1)} collective-permute-done((f32[18,64,256]{2,1,0:T(8,128)}, f32[18,64,256]{2,1,0:T(8,128)S(1)}, u32[]{:S(2)}, u32[]{:S(2)}) %collective-permute-start.4) | collective-permute-done | bytes 1179680 | tf_op jit(solution)/shard_map/ppermute | solution.py:39
  35.8 1.4 constant_dynamic-update-slice_fusion.2
  38.4 1.6 %collective-permute-start.5 = (f32[6,64,256]{2,1,0:T(8,128)S(1)}, f32[6,64,256]{2,1,0:T(8,128)S(1)}, u32[]{:S(2)}, u32[]{:S(2)}) collective-permute-start(f32[6,64,256]{2,1,0:T(8,128)S(1)} %get-tuple-element.195), channel_id=1, source_target_pairs={{0,16},{1,9},{2,18},{3,11},{4,20},{5,13},{6,22},{7,15},{8,24},{9,1... | collective-permute-start | bytes 1179656 | tf_op jit(solution)/shard_map/ppermute | solution.py:39
  40.1 8.6 %collective-permute-done.6 = f32[6,64,256]{2,1,0:T(8,128)S(1)} collective-permute-done((f32[6,64,256]{2,1,0:T(8,128)S(1)}, f32[6,64,256]{2,1,0:T(8,128)S(1)}, u32[]{:S(2)}, u32[]{:S(2)}) %collective-permute-start.6) | collective-permute-done | bytes 393248 | tf_op jit(solution)/shard_map/ppermute | solution.py:39
  49.0 1.4 collective-permute-start.7
  50.9 13.0 %collective-permute-done.8.refs_6_ = f32[7,64,256]{2,1,0:T(8,128)S(1)} collective-permute-done((f32[7,64,256]{2,1,0:T(8,128)S(1)}, f32[7,64,256]{2,1,0:T(8,128)S(1)}, u32[]{:S(2)}, u32[]{:S(2)}) %collective-permute-start.8) | collective-permute-done | bytes 458784 | tf_op jit(solution)/shard_map/ppermute | solution.py:39
  63.9 5.0 %collective-permute-done.7.refs_5_ = f32[17,64,256]{2,1,0:T(8,128)S(1)} collective-permute-done((f32[17,64,256]{2,1,0:T(8,128)S(1)}, f32[17,64,256]{2,1,0:T(8,128)S(1)}, u32[]{:S(2)}, u32[]{:S(2)}) %collective-permute-start.7) | collective-permute-done | bytes 1114144 | tf_op jit(solution)/shard_map/ppermute | solution.py:39
  69.0 1.3 shard_map.53
  70.4 1.5 shard_map.54
  72.4 1.6 %shard_map.52 = (bf16[512,768]{1,0:T(8,128)(2,1)S(1)}, f32[256,512]{1,0:T(8,128)S(1)}, bf16[512,768]{1,0:T(8,128)(2,1)S(1)}, bf16[512,1536]{1,0:T(8,128)(2,1)S(1...) custom-call(s32[11]{0:T(128)S(1)} %copy-done.5, s32[10,5]{1,0:T(8,128)S(1)} %bitcast.48, ...), custom_call_target="tpu_custom_call" | custom-call | bytes 12288 | tf_op jit(solution)/shard_map/pallas_call | solution.py:87
  76.1 1.7 %collective-permute-start.14 = (f32[10,64,128]{2,1,0:T(8,128)S(1)}, f32[10,64,128]{2,1,0:T(8,128)S(1)}, u32[]{:S(2)}, u32[]{:S(2)}) collective-permute-start(f32[10,64,128]{2,1,0:T(8,128)S(1)} %get-tuple-element.164), channel_id=1, source_target_pairs={{0,16},{1,9},{2,18},{3,11},{4,20},{5,13},{6,22},{7,15},{8,24},{9,1... | collective-permute-start | bytes 983048 | tf_op jit(solution)/shard_map/ppermute | solution.py:39
  78.5 13.7 %shard_map.55 = (f32[4,2,64,256]{3,2,1,0:T(8,128)S(1)}, f32[2,64,256]{2,1,0:T(8,128)S(1)}, f32[4,2,64,256]{3,2,1,0:T(8,128)S(1)}, f32[2,64,256]{2,1,0:T(8,128)S(1)}) custom-call(s32[11]{0:T(128)S(1)} %copy-done.5, f32[1024,512]{1,0:T(8,128)S(1)} %get-tuple-element.141.refs_1_, bf16[1536,768]{1,0:T(8,128)(2,1)S(1)} %get-tuple-element.142.refs_2_.refs_6_, ...), custom_call_target="tpu_custom_call" | custom-call | flops 125829120 | bytes 137216 | tf_op jit(solution)/shard_map/pallas_call | solution.py:87
  92.3 1.4 collective-permute-start.22
  94.4 2.2 %collective-permute-start.12 = (f32[10,64,128]{2,1,0:T(8,128)S(1)}, f32[10,64,128]{2,1,0:T(8,128)S(1)}, u32[]{:S(2)}, u32[]{:S(2)}) collective-permute-start(f32[10,64,128]{2,1,0:T(8,128)S(1)} %get-tuple-element.160), channel_id=1, source_target_pairs={{0,24},{1,25},{2,26},{3,27},{4,28},{5,29},{6,30},{7,31},{8,16},{9,... | collective-permute-start | bytes 983048 | tf_op jit(solution)/shard_map/ppermute | solution.py:39
  96.5 1.5 %collective-permute-done.15.refs_4_ = f32[10,64,128]{2,1,0:T(8,128)S(1)} collective-permute-done((f32[10,64,128]{2,1,0:T(8,128)S(1)}, f32[10,64,128]{2,1,0:T(8,128)S(1)}, u32[]{:S(2)}, u32[]{:S(2)}) %collective-permute-start.15) | collective-permute-done | bytes 327712 | tf_op jit(solution)/shard_map/ppermute | solution.py:39
  98.1 8.3 %shard_map.56 = (f32[5,2,64,128]{3,2,1,0:T(8,128)S(1)}, f32[5,2,64,128]{3,2,1,0:T(8,128)S(1)}, f32[5,2,64,128]{3,2,1,0:T(8,128)S(1)}, f32[5,2,64,128]{3,2,1,0:T(...) custom-call(s32[11]{0:T(128)S(1)} %copy-done.5, f32[10,64,128]{2,1,0:T(8,128)S(1)} %get-tuple-element.162.refs_1_, ...), custom_call_target="tpu_custom_call" | custom-call | flops 78643200 | bytes 158720 | tf_op jit(solution)/shard_map/pallas_call | solution.py:87
  106.9 11.2 %collective-permute-done.11.refs_3_ = f32[10,64,128]{2,1,0:T(8,128)S(1)} collective-permute-done((f32[10,64,128]{2,1,0:T(8,128)S(1)}, f32[10,64,128]{2,1,0:T(8,128)S(1)}, u32[]{:S(2)}, u32[]{:S(2)}) %collective-permute-start.11) | collective-permute-done | bytes 327712 | tf_op jit(solution)/shard_map/ppermute | solution.py:39
  119.2 10.0 %shard_map.57 = (f32[7,2,64,128]{3,2,1,0:T(8,128)S(1)}, f32[7,2,64,128]{3,2,1,0:T(8,128)S(1)}, f32[7,2,64,128]{3,2,1,0:T(8,128)S(1)}, f32[7,2,64,128]{3,2,1,0:T(...) custom-call(s32[11]{0:T(128)S(1)} %copy-done.5, f32[10,64,128]{2,1,0:T(8,128)S(1)} %get-tuple-element.157.refs_1_, ...), custom_call_target="tpu_custom_call" | custom-call | flops 78643200 | bytes 189440 | tf_op jit(solution)/shard_map/pallas_call | solution.py:87
  129.9 1.8 %collective-permute-start.17 = (f32[7,2,64,128]{3,2,1,0:T(8,128)S(1)}, f32[7,2,64,128]{3,2,1,0:T(8,128)S(1)}, u32[]{:S(2)}, u32[]{:S(2)}) collective-permute-start(f32[7,2,64,128]{3,2,1,0:T(8,128)S(1)} %get-tuple-element.174), channel_id=1, source_target_pairs={{0,16},{1,9},{2,18},{3,11},{4,20},{5,13},{6,22},{7,15},{8,24},{9,1... | collective-permute-start | bytes 1376264 | tf_op jit(solution)/shard_map/ppermute | solution.py:39
  132.7 13.3 %shard_map.58 = (f32[3,2,64,256]{3,2,1,0:T(8,128)S(1)}, f32[2,64,256]{2,1,0:T(8,128)S(1)}, f32[2,2,64,256]{3,2,1,0:T(8,128)S(1)}, f32[2,64,256]{2,1,0:T(8,128)S(...) custom-call(s32[11]{0:T(128)S(1)} %copy-done.5, f32[768,512]{1,0:T(8,128)S(1)} %get-tuple-element.181.refs_1_, ...), custom_call_target="tpu_custom_call" | custom-call | flops 125829120 | bytes 92160 | tf_op jit(solution)/shard_map/pallas_call | solution.py:87
  146.1 2.6 %shard_map.59.refs_5_ = f32[1,10,5,2,64,256]{5,4,3,2,1,0:T(8,128)} custom-call(s32[11]{0:T(128)S(1)} %copy-done.5, f32[1,2,64,256]{3,2,1,0:T(8,128)S(1)} %get-tuple-element.184.refs_1_, f32[2,2,64,256]{3,2,1,0:T(8,128)S(1)} %get-tuple-element.185.refs_2_, f32[3,2,64,256]{3,2,1,0:T(8,128)S(1)} %get-tuple-element.186.refs_3_, ...), custom_call_target="tpu_custom_call" | custom-call | bytes 7168 | tf_op jit(solution)/shard_map/pallas_call | solution.py:87
  148.7 1.6 %shard_map.60.refs_5_ = f32[1,10,5,2,64,256]{5,4,3,2,1,0:T(8,128)} custom-call(s32[11]{0:T(128)S(1)} %copy-done.5, f32[5,2,64,128]{3,2,1,0:T(8,128)S(1)} %get-tuple-element.176.refs_1_, f32[5,2,64,128]{3,2,1,0:T(8,128)S(1)} %collective-permute-done.19.refs_2_, f32[5,2,64,128]{3,2,1,0:T(8,128)S(1)} %collective-permute-done.20.refs_3_, ...), custom_call_target="tpu_custom_call", output_to_operand_aliasing={{}: (5, {})} | custom-call | bytes 30720 | tf_op jit(solution)/shard_map/pallas_call | solution.py:87
  150.8 2.7 %shard_map.61 = (f32[1,10,5,2,64,256]{5,4,3,2,1,0:T(8,128)}, f32[1,10,2,64,256]{4,3,2,1,0:T(8,128)}) custom-call(s32[11]{0:T(128)S(1)} %copy-done.5, f32[7,2,64,128]{3,2,1,0:T(8,128)S(1)} %get-tuple-element.172.refs_1_, f32[7,2,64,128]{3,2,1,0:T(8,128)S(1)} %collective-permute-done.16.refs_2_, ...), custom_call_target="tpu_custom_call", output_to_operand_aliasing={{0}: (5, {})} | custom-call | bytes 40448 | tf_op jit(solution)/shard_map/pallas_call | solution.py:87
  (70 shorter events, 17.2 us)
Async XLA Ops:
  4.8 10.9 %copy-start.7 = (s32[1,10,5]{1,0,2:T(1,128)S(1)}, s32[1,10,5]{1,0,2:T(1,128)}, u32[]{:S(2)}) copy-start(s32[1,10,5]{1,0,2:T(1,128)} %param.5) | copy-start | bytes 604
  6.1 29.7 %collective-permute-start.4 = (f32[18,64,256]{2,1,0:T(8,128)}, f32[18,64,256]{2,1,0:T(8,128)S(1)}, u32[]{:S(2)}, u32[]{:S(2)}) collective-permute-start(f32[18,64,256]{2,1,0:T(8,128)} %get-tuple-element.202), channel_id=1, source_target_pairs={{0,16},{1,9},{2,18},{3,11},{4,20},{5,13},{6,22},{7,15},{8,24},{9,1... | collective-permute-start | bytes 3538952 | tf_op jit(solution)/shard_map/ppermute | solution.py:39
  9.1 26.8 %collective-permute-start.3 = (f32[18,64,256]{2,1,0:T(8,128)S(1)}, f32[18,64,256]{2,1,0:T(8,128)S(1)}, u32[]{:S(2)}, u32[]{:S(2)}) collective-permute-start(f32[18,64,256]{2,1,0:T(8,128)S(1)} %get-tuple-element.203.refs_2_), channel_id=1, source_target_pairs={{0,8},{1,17},{2,10},{3,19},{4,12},{5,21},{6,14},{7,23},{8,0},{9,25... | collective-permute-start | bytes 3538952 | tf_op jit(solution)/shard_map/ppermute | solution.py:39
  10.5 10.7 %collective-permute-start = (f32[2,64,256]{2,1,0:T(8,128)}, f32[2,64,256]{2,1,0:T(8,128)}, u32[]{:S(2)}, u32[]{:S(2)}) collective-permute-start(f32[2,64,256]{2,1,0:T(8,128)} %get-tuple-element.201), channel_id=1, source_target_pairs={{0,4},{8,12},{16,20},{24,28}} | collective-permute-start | bytes 393224 | tf_op jit(solution)/shard_map/ppermute | solution.py:536
  20.2 6.8 %copy-start.4 = (s32[1,10,5]{2,1,0:T(8,128)S(1)}, s32[1,10,5]{2,1,0:T(8,128)}, u32[]{:S(2)}) copy-start(s32[1,10,5]{2,1,0:T(8,128)} %copy.23) | copy-start | bytes 604
  20.3 6.8 %copy-start.5 = (s32[11]{0:T(128)S(1)}, s32[11]{0:T(128)}, u32[]{:S(2)}) copy-start(s32[11]{0:T(128)} %stack.54.refs_0_) | copy-start | bytes 136
  23.0 8.0 %collective-permute-start.2 = (f32[6,64,256]{2,1,0:T(8,128)}, f32[6,64,256]{2,1,0:T(8,128)}, u32[]{:S(2)}, u32[]{:S(2)}) collective-permute-start(f32[6,64,256]{2,1,0:T(8,128)} %pad_maximum_fusion.5), channel_id=1, source_target_pairs={{0,3},{4,7},{8,11},{12,15},{16,19},{20,23},{24,27},{28,31}} | collective-permute-start | bytes 1179656 | tf_op jit(solution)/shard_map/ppermute | solution.py:545
  25.0 6.0 %collective-permute-start.1 = (f32[6,64,256]{2,1,0:T(8,128)}, f32[6,64,256]{2,1,0:T(8,128)}, u32[]{:S(2)}, u32[]{:S(2)}) collective-permute-start(f32[6,64,256]{2,1,0:T(8,128)} %pad_maximum_fusion.5), channel_id=1, source_target_pairs={{0,1},{4,5},{8,9},{12,13},{16,17},{20,21},{24,25},{28,29}} | collective-permute-start | bytes 1179656 | tf_op jit(solution)/shard_map/ppermute | solution.py:542
  27.1 2.9 %copy-start = (f32[1,10,5,2,64,256]{5,4,3,2,1,0:T(8,128)S(1)}, f32[1,10,5,2,64,256]{5,4,3,2,1,0:T(8,128)}, u32[]{:S(2)}) copy-start(f32[1,10,5,2,64,256]{5,4,3,2,1,0:T(8,128)} %refs_2_.3) | copy-start | bytes 19660804
  31.0 4.9 %copy-start.6 = (f32[6,64,256]{2,1,0:T(8,128)S(1)}, f32[6,64,256]{2,1,0:T(8,128)}, u32[]{:S(2)}) copy-start(f32[6,64,256]{2,1,0:T(8,128)} %get-tuple-element.101) | copy-start | bytes 1179652
  37.2 2.9 %slice-start = ((f32[18,64,256]{2,1,0:T(8,128)}), f32[8,64,256]{2,1,0:T(8,128)S(1)}, s32[]{:S(2)}) async-start(f32[18,64,256]{2,1,0:T(8,128)} %copy-done.1), calls=%async_computation | async-start | bytes 1048576 | tf_op jit(solution)/shard_map/slice | solution.py:577
  37.2 11.5 %collective-permute-start.6 = (f32[6,64,256]{2,1,0:T(8,128)S(1)}, f32[6,64,256]{2,1,0:T(8,128)S(1)}, u32[]{:S(2)}, u32[]{:S(2)}) collective-permute-start(f32[6,64,256]{2,1,0:T(8,128)S(1)} %get-tuple-element.195), channel_id=1, source_target_pairs={{0,8},{1,17},{2,10},{3,19},{4,12},{5,21},{6,14},{7,23},{8,0},{9,25... | collective-permute-start | bytes 1179656 | tf_op jit(solution)/shard_map/ppermute | solution.py:39
  38.4 10.4 %collective-permute-start.5 = (f32[6,64,256]{2,1,0:T(8,128)S(1)}, f32[6,64,256]{2,1,0:T(8,128)S(1)}, u32[]{:S(2)}, u32[]{:S(2)}) collective-permute-start(f32[6,64,256]{2,1,0:T(8,128)S(1)} %get-tuple-element.195), channel_id=1, source_target_pairs={{0,16},{1,9},{2,18},{3,11},{4,20},{5,13},{6,22},{7,15},{8,24},{9,1... | collective-permute-start | bytes 1179656 | tf_op jit(solution)/shard_map/ppermute | solution.py:39
  40.0 8.8 %slice-start.1 = ((f32[18,64,256]{2,1,0:T(8,128)}), f32[10,64,256]{2,1,0:T(8,128)S(1)}, s32[]{:S(2)}) async-start(f32[18,64,256]{2,1,0:T(8,128)} %copy-done.1), calls=%async_computation.1 | async-start | bytes 1310720 | tf_op jit(solution)/shard_map/slice | solution.py:582
  49.0 20.1 %copy-start.2 = (f32[18,64,256]{2,1,0:T(8,128)S(1)}, f32[18,64,256]{2,1,0:T(8,128)}, u32[]{:S(2)}) copy-start(f32[18,64,256]{2,1,0:T(8,128)} %copy-done.1) | copy-start | bytes 3538948
  49.0 19.9 %collective-permute-start.7 = (f32[17,64,256]{2,1,0:T(8,128)S(1)}, f32[17,64,256]{2,1,0:T(8,128)S(1)}, u32[]{:S(2)}, u32[]{:S(2)}) collective-permute-start(f32[17,64,256]{2,1,0:T(8,128)S(1)} %pad_maximum_fusion.2), channel_id=1, source_target_pairs={{0,8},{1,17},{2,10},{3,19},{4,12},{5,21},{6,14},{7,23},{8,0},{9,25... | collective-permute-start | bytes 3342344 | tf_op jit(solution)/shard_map/ppermute | solution.py:39
  50.4 13.5 %collective-permute-start.8 = (f32[7,64,256]{2,1,0:T(8,128)S(1)}, f32[7,64,256]{2,1,0:T(8,128)S(1)}, u32[]{:S(2)}, u32[]{:S(2)}) collective-permute-start(f32[7,64,256]{2,1,0:T(8,128)S(1)} %pad_maximum_fusion.4), channel_id=1, source_target_pairs={{0,16},{1,9},{2,18},{3,11},{4,20},{5,13},{6,22},{7,15},{8,24},{9,1... | collective-permute-start | bytes 1376264 | tf_op jit(solution)/shard_map/ppermute | solution.py:39
  68.9 3.5 %collective-permute-start.9 = (f32[24,64,256]{2,1,0:T(8,128)S(1)}, f32[24,64,256]{2,1,0:T(8,128)S(1)}, u32[]{:S(2)}, u32[]{:S(2)}) collective-permute-start(f32[24,64,256]{2,1,0:T(8,128)S(1)} %slice_dynamic-update-slice_fusion.refs_2_), channel_id=1, source_target_pairs={{0,1},{1,0},{2,3},{3,2},{4,5},{5,4},{6,7},{7,6},{8,9},{9,8},{10,11... | collective-permute-start | bytes 4718600 | tf_op jit(solution)/shard_map/ppermute | solution.py:29
  74.0 18.2 %collective-permute-start.10 = (f32[10,64,128]{2,1,0:T(8,128)S(1)}, f32[10,64,128]{2,1,0:T(8,128)S(1)}, u32[]{:S(2)}, u32[]{:S(2)}) collective-permute-start(f32[10,64,128]{2,1,0:T(8,128)S(1)} %get-tuple-element.155), channel_id=1, source_target_pairs={{0,8},{1,17},{2,10},{3,19},{4,12},{5,21},{6,14},{7,23},{8,0},{9,25... | collective-permute-start | bytes 983048 | tf_op jit(solution)/shard_map/ppermute | solution.py:39
  75.0 19.3 %collective-permute-start.13 = (f32[10,64,128]{2,1,0:T(8,128)S(1)}, f32[10,64,128]{2,1,0:T(8,128)S(1)}, u32[]{:S(2)}, u32[]{:S(2)}) collective-permute-start(f32[10,64,128]{2,1,0:T(8,128)S(1)} %get-tuple-element.163), channel_id=1, source_target_pairs={{0,8},{1,17},{2,10},{3,19},{4,12},{5,21},{6,14},{7,23},{8,0},{9,25... | collective-permute-start | bytes 983048 | tf_op jit(solution)/shard_map/ppermute | solution.py:39
  76.1 20.4 %collective-permute-start.14 = (f32[10,64,128]{2,1,0:T(8,128)S(1)}, f32[10,64,128]{2,1,0:T(8,128)S(1)}, u32[]{:S(2)}, u32[]{:S(2)}) collective-permute-start(f32[10,64,128]{2,1,0:T(8,128)S(1)} %get-tuple-element.164), channel_id=1, source_target_pairs={{0,16},{1,9},{2,18},{3,11},{4,20},{5,13},{6,22},{7,15},{8,24},{9,1... | collective-permute-start | bytes 983048 | tf_op jit(solution)/shard_map/ppermute | solution.py:39
  77.8 20.3 %collective-permute-start.15 = (f32[10,64,128]{2,1,0:T(8,128)S(1)}, f32[10,64,128]{2,1,0:T(8,128)S(1)}, u32[]{:S(2)}, u32[]{:S(2)}) collective-permute-start(f32[10,64,128]{2,1,0:T(8,128)S(1)} %get-tuple-element.165), channel_id=1, source_target_pairs={{0,24},{1,25},{2,26},{3,27},{4,28},{5,29},{6,30},{7,31},{8,16},{9,... | collective-permute-start | bytes 983048 | tf_op jit(solution)/shard_map/ppermute | solution.py:39
  92.3 39.3 %collective-permute-start.22 = (f32[5,2,64,256]{3,2,1,0:T(8,128)S(1)}, f32[5,2,64,256]{3,2,1,0:T(8,128)S(1)}, u32[]{:S(2)}, u32[]{:S(2)}) collective-permute-start(f32[5,2,64,256]{3,2,1,0:T(8,128)S(1)} %pad_maximum_fusion.3), channel_id=1, source_target_pairs={{0,16},{1,9},{2,18},{3,11},{4,20},{5,13},{6,22},{7,15},{8,24},{9,1... | collective-permute-start | bytes 1966088 | tf_op jit(solution)/shard_map/ppermute | solution.py:39
  93.7 24.4 %collective-permute-start.11 = (f32[10,64,128]{2,1,0:T(8,128)S(1)}, f32[10,64,128]{2,1,0:T(8,128)S(1)}, u32[]{:S(2)}, u32[]{:S(2)}) collective-permute-start(f32[10,64,128]{2,1,0:T(8,128)S(1)} %get-tuple-element.159), channel_id=1, source_target_pairs={{0,16},{1,9},{2,18},{3,11},{4,20},{5,13},{6,22},{7,15},{8,24},{9,1... | collective-permute-start | bytes 983048 | tf_op jit(solution)/shard_map/ppermute | solution.py:39
  94.4 24.8 %collective-permute-start.12 = (f32[10,64,128]{2,1,0:T(8,128)S(1)}, f32[10,64,128]{2,1,0:T(8,128)S(1)}, u32[]{:S(2)}, u32[]{:S(2)}) collective-permute-start(f32[10,64,128]{2,1,0:T(8,128)S(1)} %get-tuple-element.160), channel_id=1, source_target_pairs={{0,24},{1,25},{2,26},{3,27},{4,28},{5,29},{6,30},{7,31},{8,16},{9,... | collective-permute-start | bytes 983048 | tf_op jit(solution)/shard_map/ppermute | solution.py:39
  106.4 23.4 %collective-permute-start.19 = (f32[5,2,64,128]{3,2,1,0:T(8,128)S(1)}, f32[5,2,64,128]{3,2,1,0:T(8,128)S(1)}, u32[]{:S(2)}, u32[]{:S(2)}) collective-permute-start(f32[5,2,64,128]{3,2,1,0:T(8,128)S(1)} %get-tuple-element.177), channel_id=1, source_target_pairs={{0,8},{1,17},{2,10},{3,19},{4,12},{5,21},{6,14},{7,23},{8,0},{9,25... | collective-permute-start | bytes 983048 | tf_op jit(solution)/shard_map/ppermute | solution.py:39
  106.9 41.8 %collective-permute-start.20 = (f32[5,2,64,128]{3,2,1,0:T(8,128)S(1)}, f32[5,2,64,128]{3,2,1,0:T(8,128)S(1)}, u32[]{:S(2)}, u32[]{:S(2)}) collective-permute-start(f32[5,2,64,128]{3,2,1,0:T(8,128)S(1)} %get-tuple-element.178), channel_id=1, source_target_pairs={{0,16},{1,9},{2,18},{3,11},{4,20},{5,13},{6,22},{7,15},{8,24},{9,1... | collective-permute-start | bytes 983048 | tf_op jit(solution)/shard_map/ppermute | solution.py:39
  118.1 30.6 %collective-permute-start.21 = (f32[5,2,64,128]{3,2,1,0:T(8,128)S(1)}, f32[5,2,64,128]{3,2,1,0:T(8,128)S(1)}, u32[]{:S(2)}, u32[]{:S(2)}) collective-permute-start(f32[5,2,64,128]{3,2,1,0:T(8,128)S(1)} %get-tuple-element.179), channel_id=1, source_target_pairs={{0,24},{1,25},{2,26},{3,27},{4,28},{5,29},{6,30},{7,31},{8,16},{9,... | collective-permute-start | bytes 983048 | tf_op jit(solution)/shard_map/ppermute | solution.py:39
  129.2 21.2 %collective-permute-start.16 = (f32[7,2,64,128]{3,2,1,0:T(8,128)S(1)}, f32[7,2,64,128]{3,2,1,0:T(8,128)S(1)}, u32[]{:S(2)}, u32[]{:S(2)}) collective-permute-start(f32[7,2,64,128]{3,2,1,0:T(8,128)S(1)} %get-tuple-element.173), channel_id=1, source_target_pairs={{0,8},{1,17},{2,10},{3,19},{4,12},{5,21},{6,14},{7,23},{8,0},{9,25... | collective-permute-start | bytes 1376264 | tf_op jit(solution)/shard_map/ppermute | solution.py:39
  129.9 20.5 %collective-permute-start.17 = (f32[7,2,64,128]{3,2,1,0:T(8,128)S(1)}, f32[7,2,64,128]{3,2,1,0:T(8,128)S(1)}, u32[]{:S(2)}, u32[]{:S(2)}) collective-permute-start(f32[7,2,64,128]{3,2,1,0:T(8,128)S(1)} %get-tuple-element.174), channel_id=1, source_target_pairs={{0,16},{1,9},{2,18},{3,11},{4,20},{5,13},{6,22},{7,15},{8,24},{9,1... | collective-permute-start | bytes 1376264 | tf_op jit(solution)/shard_map/ppermute | solution.py:39
  131.6 19.2 %collective-permute-start.18 = (f32[7,2,64,128]{3,2,1,0:T(8,128)S(1)}, f32[7,2,64,128]{3,2,1,0:T(8,128)S(1)}, u32[]{:S(2)}, u32[]{:S(2)}) collective-permute-start(f32[7,2,64,128]{3,2,1,0:T(8,128)S(1)} %get-tuple-element.175), channel_id=1, source_target_pairs={{0,24},{1,25},{2,26},{3,27},{4,28},{5,29},{6,30},{7,31},{8,16},{9,... | collective-permute-start | bytes 1376264 | tf_op jit(solution)/shard_map/ppermute | solution.py:39
  148.7 2.1 %copy-start.3 = (f32[1,10,2,64,256]{4,3,2,1,0:T(8,128)S(1)}, f32[1,10,2,64,256]{4,3,2,1,0:T(8,128)}, u32[]{:S(2)}) copy-start(f32[1,10,2,64,256]{4,3,2,1,0:T(8,128)} %refs_6_.1) | copy-start | bytes 3932164
  (1 other events, 1.4 us)
where the time goes:
time: 154 us
  Pallas kernels  61 us (40%)
  waiting for transfers between devices  45.2 us (29%)
  starting transfers between devices  32.1 us (21%)
  local copies, waits for them, and re-layouts  9.56 us (6%)
  other arithmetic  4.54 us (3%)
    pallas_call x12, Pallas kernels, run_kernel(): pl.pallas_call(kernel, out_shape=[jax.ShapeDtypeStruct(shape, dtype) for...  61 us
    ppermute x19, waiting for transfers between devices, row_swap(): return lax.ppermute(value, ('row', 'col'), pairs)  44.6 us
    ppermute x19, starting transfers between devices, row_swap(): return lax.ppermute(value, ('row', 'col'), pairs)  22.8 us
    ppermute x1, starting transfers between devices, body(): arrived = lax.ppermute(travelling, 'col', pairs)  5.13 us
  transfers between devices with their start and end apart: 23, of which 8 were waited for; matrix products, arithmetic and copies ran while one was open for 3% of the time, Pallas kernels for 37%

commit v1 on v0

--- a/solution.py
+++ b/solution.py
@@ -440,13 +440,14 @@
         copy.wait()
 
 
-def place_kernel(plan, depth, cols, half, diag_plan, shared, *refs):
+def place_kernel(plan, depth, cols, half, late_plan, diag_plan, shared, *refs):
     refs = list(refs)
     scalars = refs.pop(0)
     pieces = [refs.pop(0) for _ in plan]
     refs.pop(0)
     last_half = half + 1 == HALVES
     own = refs.pop(0) if last_half else None
+    late = [refs.pop(0) for _ in late_plan] if last_half else []
     corrections = [refs.pop(0) for _ in diag_plan] if last_half else []
     out = refs.pop(0)
     diag = refs.pop(0) if last_half else None
@@ -456,6 +457,9 @@
     for at, (piece, slot) in enumerate(zip(pieces, slots)):
         target = out.at[0, slot, :, :, :, pl.ds(half * cols, cols)]
         copies.append(pltpu.make_async_copy(piece.at[pl.ds(0, depth)], target, sem.at[at]))
+    for piece, (slot, level) in zip(late, late_plan):
+        target = out.at[0, slot, pl.ds(0, level)]
+        copies.append(pltpu.make_async_copy(piece, target, sem.at[len(copies)]))
     for copy in copies:
         copy.start()
     if last_half:
@@ -567,29 +571,31 @@
     def halves(value):
         return value.reshape(value.shape[0] // 2, 2, chunk, width)
 
-    near_sends, far_sends = [halves(far)[:, 0]], [halves(near)[:, 1]]
+    near_sends, far_sends, pair_sends = [halves(far)[:, 0]], [halves(near)[:, 1]], []
     homes = {}
-    near_size = far_size = planes // 2
+    size, pair_size = planes // 2, 0
     for depth in middle:
         first, count = 2 * bases[depth], 2 * (depth + 1)
-        homes[depth] = (near_size, far_size)
         if groups[depth] > 2:
+            homes[depth] = size
             near_sends.append(halves(far_got[first : first + count])[:, 0])
             far_sends.append(halves(near_got[first : first + count])[:, 1])
-            near_size += depth + 1
-            far_size += depth + 1
+            size += depth + 1
         else:
-            near_sends.append(far_got[first : first + count])
-            near_size += count
+            homes[depth] = pair_size
+            pair_sends.append(far_got[first : first + count])
+            pair_size += count
     near_sends = jnp.concatenate(near_sends, axis=0)
     far_sends = jnp.concatenate(far_sends, axis=0)
+    pair_sends = [jnp.concatenate(pair_sends, axis=0)] if pair_sends else []
     nodes, group = per_col[last], groups[last]
     last_packs = pack_last(
         offsets[last], nodes, last, [(step, group) for step in range(nodes)], cols,
         scalars, present, lower_panel,
     )
-    near_sends, far_sends, last_packs = lax.optimization_barrier(
-        (near_sends, far_sends, last_packs)
+    pair_more = [row_swap(value, 1) for value in pair_sends]
+    near_sends, far_sends, pair_more, last_packs = lax.optimization_barrier(
+        (near_sends, far_sends, pair_more, last_packs)
     )
     near_more = row_swap(near_sends, 1)
     far_more = row_swap(far_sends, 2)
@@ -608,13 +614,13 @@
     made = {}
     for depth in middle:
         base = bases[depth]
-        near_home, far_home = homes[depth]
+        home = homes[depth]
         pieces = both_parts(0, near_pack, base) + both_parts(1, near_got, base)
         pieces += both_parts(2, far_got, base)
         if groups[depth] > 2:
-            pieces += [(3, 0, near_more, near_home, 1), (3, 1, far_more, far_home, 1)]
+            pieces += [(3, 0, near_more, home, 1), (3, 1, far_more, home, 1)]
         else:
-            pieces += [(3, 0, near_more, near_home, 2), (3, 1, near_more, near_home + 1, 2)]
+            pieces += [(3, 0, pair_more[0], home, 2), (3, 1, pair_more[0], home + 1, 2)]
         level = (depth, None, 0, (offsets[depth], groups[depth]))
         made.update(prep([level], pieces, scalars, present, rows, chunk, width))
     levels = [(depth, True, starts[at], None) for at, depth in enumerate(upper)]
@@ -646,10 +652,10 @@
     for depth in range(1, last):
         if per_col[depth] > 1:
             solved.update(solve([depth], made, scalars, steps[depth], chunk, width, ()))
-    second = [value for _, value in last_pieces[-1][:2]]
+    second = [value for _, value in last_pieces[-1][:-1]]
     solved, second, later = lax.optimization_barrier((solved, second, scalars))
-    last_pieces[-1][:2] = [
-        (at, value) for (at, _), value in zip(last_pieces[-1][:2], second)
+    last_pieces[-1][:-1] = [
+        (at, value) for (at, _), value in zip(last_pieces[-1][:-1], second)
     ]
     lefts, backs = [], []
     for half in range(HALVES):
@@ -666,14 +672,19 @@
     solved.update(solve(single, made, later, [0], chunk, width, tuple(shared)))
 
     begin_plan, begin_pieces, diag_plan, diag_pieces = [], [], [], []
+    late_plan, late_pieces = [], []
     for depth in range(1, last):
         for step, (piece, correction) in enumerate(solved[depth]):
             if step:
                 both = jnp.concatenate([piece, correction[None]], axis=0)
                 both = row_swap(both, steps[depth][step])
                 piece, correction = both[:depth], both[depth]
-            begin_plan.append((offsets[depth], groups[depth], step, depth))
-            begin_pieces.append(piece)
+            if per_col[depth] == 1:
+                late_plan.append((offsets[depth], depth))
+                late_pieces.append(piece)
+            else:
+                begin_plan.append((offsets[depth], groups[depth], step, depth))
+                begin_pieces.append(piece)
             diag_plan.append((offsets[depth], groups[depth], step))
             diag_pieces.append(correction)
     zeros = [
@@ -699,13 +710,16 @@
         ins = [(scalars, SMEM)] + [(piece, VMEM) for piece in back] + [(sel_panel, ANY)]
         outs = [(panel_shape, F32, ANY)]
         if half + 1 == HALVES:
-            ins += [(diag_inverse, VMEM)] + [(piece, VMEM) for piece in diag_pieces]
+            ins += [(diag_inverse, VMEM)]
+            ins += [(piece, VMEM) for piece in late_pieces + diag_pieces]
             outs.append((diag_inverse.shape, F32, VMEM))
         made_now = run_kernel(
-            functools.partial(place_kernel, last_plan, last, cols, half, diag_plan, masked),
+            functools.partial(
+                place_kernel, last_plan, last, cols, half, late_plan, diag_plan, masked
+            ),
             outs,
             ins,
-            [pltpu.SemaphoreType.DMA((nodes,))],
+            [pltpu.SemaphoreType.DMA((nodes + len(late_plan),))],
             0,
             aliases={1 + nodes: 0},
         )

time: 154 us -> 150 us (0.974)
  waiting for transfers between devices: 45.2 us -> 36.7 us
  starting transfers between devices: 32.1 us -> 34.4 us
    ppermute x19 -> x20, waiting for transfers between devices: 44.6 us -> 36.7 us  [row_swap(): return lax.ppermute(value, ('row', 'col'), pairs)]
    ppermute x19 -> x20, starting transfers between devices: 22.8 us -> 25.1 us  [row_swap(): return lax.ppermute(value, ('row', 'col'), pairs)]
    unnamed x19 -> x23, local copies, waits for them, and re-layouts: 2.96 us -> 4.11 us
  transfers between devices with their start and end apart: 23 -> 24, of which waited for: 8 -> 7; matrix products, arithmetic and copies ran while one was open for 3% -> 3% of each run, Pallas kernels for 37% -> 38%
where the time goes in v1:
time: 150 us; the launch traced here: 149 us
  Pallas kernels  61 us (41%)
  waiting for transfers between devices  36.7 us (24%)
  starting transfers between devices  34.4 us (23%)
  local copies, waits for them, and re-layouts  10.8 us (7%)
  other arithmetic  4.47 us (3%)
    pallas_call x12, Pallas kernels, run_kernel(): pl.pallas_call(kernel, out_shape=[jax.ShapeDtypeStruct(shape, dtype) for...  61 us
    ppermute x20, waiting for transfers between devices, row_swap(): return lax.ppermute(value, ('row', 'col'), pairs)  36.7 us
    ppermute x20, starting transfers between devices, row_swap(): return lax.ppermute(value, ('row', 'col'), pairs)  25.1 us
    ppermute x1, starting transfers between devices, body(): arrived = lax.ppermute(travelling, 'col', pairs)  5.14 us
    unnamed x23, local copies, waits for them, and re-layouts  4.11 us
  transfers between devices with their start and end apart: 24, of which 7 were waited for; matrix products, arithmetic and copies ran while one was open for 3% of the time, Pallas kernels for 38%

profile of v1, /device:TPU:0, one launch (start us, length us, event | category | flops | bytes accessed | tf_op | source)
XLA Modules:
  0.0 148.6 jit_solution(881290567009251857)
XLA Ops:
  3.0 1.8 %dynamic-slice_bitcast_fusion = (f32[2,64,256]{2,1,0:T(8,128)S(1)}, f32[2,64,256]{2,1,0:T(8,128)S(1)}, f32[2,64,256]{2,1,0:T(8,128)S(1)}, f32[2,64,256]{2,1,0:T(8,128)}) fusion(f32[1,10,2,64,256]{4,3,2,1,0:T(8,128)} %refs_6_.1, s32[]{:T(128)S(6)} %select_n.99, s32[]{:T(128)S(6)} %select_n.98, s32[]{:T(128)S(6)} %select_n.96), kind=kLoop, calls=%fused_computation.16 | loop fusion | bytes 1048588 | tf_op jit(solution)/shard_map/jit(dynamic_index_in_dim)/squeeze | solution.py:525
  6.1 3.0 %collective-permute-start.4 = (f32[18,64,256]{2,1,0:T(8,128)}, f32[18,64,256]{2,1,0:T(8,128)S(1)}, u32[]{:S(2)}, u32[]{:S(2)}) collective-permute-start(f32[18,64,256]{2,1,0:T(8,128)} %get-tuple-element.206), channel_id=1, source_target_pairs={{0,16},{1,9},{2,18},{3,11},{4,20},{5,13},{6,22},{7,15},{8,24},{9,1... | collective-permute-start | bytes 3538952 | tf_op jit(solution)/shard_map/ppermute | solution.py:39
  9.1 1.5 %collective-permute-start.3 = (f32[18,64,256]{2,1,0:T(8,128)S(1)}, f32[18,64,256]{2,1,0:T(8,128)S(1)}, u32[]{:S(2)}, u32[]{:S(2)}) collective-permute-start(f32[18,64,256]{2,1,0:T(8,128)S(1)} %get-tuple-element.207.refs_2_), channel_id=1, source_target_pairs={{0,8},{1,17},{2,10},{3,19},{4,12},{5,21},{6,14},{7,23},{8,0},{9,25... | collective-permute-start | bytes 3538952 | tf_op jit(solution)/shard_map/ppermute | solution.py:39
  10.5 5.1 %collective-permute-start = (f32[2,64,256]{2,1,0:T(8,128)}, f32[2,64,256]{2,1,0:T(8,128)}, u32[]{:S(2)}, u32[]{:S(2)}) collective-permute-start(f32[2,64,256]{2,1,0:T(8,128)} %get-tuple-element.205), channel_id=1, source_target_pairs={{0,4},{8,12},{16,20},{24,28}} | collective-permute-start | bytes 393224 | tf_op jit(solution)/shard_map/ppermute | solution.py:540
  17.0 3.2 %shard_map.50 = (f32[6,64,256]{2,1,0:T(8,128)}, f32[6,64,256]{2,1,0:T(8,128)}) custom-call(s32[11]{0:T(128)} %stack.54.refs_0_, s32[10,5]{1,0:T(8,128)} %bitcast.44, f32[1,10,5,2,64,256]{5,4,3,2,1,0:T(8,128)} %refs_2_.3, f32[1,10,2,64,256]{4,3,2,1,0:T(8,128)} %refs_6_.1), custom_call_target="tpu_custom_call" | custom-call | bytes 30720 | tf_op jit(solution)/shard_map/pallas_call | solution.py:87
  23.0 2.0 %collective-permute-start.2 = (f32[6,64,256]{2,1,0:T(8,128)}, f32[6,64,256]{2,1,0:T(8,128)}, u32[]{:S(2)}, u32[]{:S(2)}) collective-permute-start(f32[6,64,256]{2,1,0:T(8,128)} %pad_maximum_fusion.5), channel_id=1, source_target_pairs={{0,3},{4,7},{8,11},{12,15},{16,19},{20,23},{24,27},{28,31}} | collective-permute-start | bytes 1179656 | tf_op jit(solution)/shard_map/ppermute | solution.py:549
  25.0 2.1 %collective-permute-start.1 = (f32[6,64,256]{2,1,0:T(8,128)}, f32[6,64,256]{2,1,0:T(8,128)}, u32[]{:S(2)}, u32[]{:S(2)}) collective-permute-start(f32[6,64,256]{2,1,0:T(8,128)} %pad_maximum_fusion.5), channel_id=1, source_target_pairs={{0,1},{4,5},{8,9},{12,13},{16,17},{20,21},{24,25},{28,29}} | collective-permute-start | bytes 1179656 | tf_op jit(solution)/shard_map/ppermute | solution.py:546
  27.1 2.9 %copy-done = f32[1,10,5,2,64,256]{5,4,3,2,1,0:T(8,128)S(1)} copy-done((f32[1,10,5,2,64,256]{5,4,3,2,1,0:T(8,128)S(1)}, f32[1,10,5,2,64,256]{5,4,3,2,1,0:T(8,128)}, u32[]{:S(2)}) %copy-start) | copy-done | bytes 6553624
  31.0 4.8 %collective-permute-done.4.refs_4_ = f32[18,64,256]{2,1,0:T(8,128)S(1)} collective-permute-done((f32[18,64,256]{2,1,0:T(8,128)}, f32[18,64,256]{2,1,0:T(8,128)S(1)}, u32[]{:S(2)}, u32[]{:S(2)}) %collective-permute-start.4) | collective-permute-done | bytes 1179680 | tf_op jit(solution)/shard_map/ppermute | solution.py:39
  38.4 1.7 %collective-permute-start.5 = (f32[6,64,256]{2,1,0:T(8,128)S(1)}, f32[6,64,256]{2,1,0:T(8,128)S(1)}, u32[]{:S(2)}, u32[]{:S(2)}) collective-permute-start(f32[6,64,256]{2,1,0:T(8,128)S(1)} %get-tuple-element.199), channel_id=1, source_target_pairs={{0,16},{1,9},{2,18},{3,11},{4,20},{5,13},{6,22},{7,15},{8,24},{9,1... | collective-permute-start | bytes 1179656 | tf_op jit(solution)/shard_map/ppermute | solution.py:39
  40.1 1.6 %collective-permute-start.7 = (f32[10,64,256]{2,1,0:T(8,128)S(1)}, f32[10,64,256]{2,1,0:T(8,128)S(1)}, u32[]{:S(2)}, u32[]{:S(2)}) collective-permute-start(f32[10,64,256]{2,1,0:T(8,128)S(1)} %slice.67), channel_id=1, source_target_pairs={{0,8},{1,17},{2,10},{3,19},{4,12},{5,21},{6,14},{7,23},{8,0},{9,25... | collective-permute-start | bytes 1966088 | tf_op jit(solution)/shard_map/ppermute | solution.py:39
  41.7 7.1 %collective-permute-done.6 = f32[6,64,256]{2,1,0:T(8,128)S(1)} collective-permute-done((f32[6,64,256]{2,1,0:T(8,128)S(1)}, f32[6,64,256]{2,1,0:T(8,128)S(1)}, u32[]{:S(2)}, u32[]{:S(2)}) %collective-permute-start.6) | collective-permute-done | bytes 393248 | tf_op jit(solution)/shard_map/ppermute | solution.py:39
  48.8 1.6 %collective-permute-done.5 = f32[6,64,256]{2,1,0:T(8,128)S(1)} collective-permute-done((f32[6,64,256]{2,1,0:T(8,128)S(1)}, f32[6,64,256]{2,1,0:T(8,128)S(1)}, u32[]{:S(2)}, u32[]{:S(2)}) %collective-permute-start.5) | collective-permute-done | bytes 393248 | tf_op jit(solution)/shard_map/ppermute | solution.py:39
  50.5 5.9 %collective-permute-done.7.refs_5_ = f32[10,64,256]{2,1,0:T(8,128)S(1)} collective-permute-done((f32[10,64,256]{2,1,0:T(8,128)S(1)}, f32[10,64,256]{2,1,0:T(8,128)S(1)}, u32[]{:S(2)}, u32[]{:S(2)}) %collective-permute-start.7) | collective-permute-done | bytes 655392 | tf_op jit(solution)/shard_map/ppermute | solution.py:39
  57.7 11.8 %collective-permute-done.8.refs_5_ = f32[7,64,256]{2,1,0:T(8,128)S(1)} collective-permute-done((f32[7,64,256]{2,1,0:T(8,128)S(1)}, f32[7,64,256]{2,1,0:T(8,128)S(1)}, u32[]{:S(2)}, u32[]{:S(2)}) %collective-permute-start.8) | collective-permute-done | bytes 458784 | tf_op jit(solution)/shard_map/ppermute | solution.py:39
  69.6 1.5 %shard_map.54 = (f32[1024,512]{1,0:T(8,128)S(1)}, bf16[2048,768]{1,0:T(8,128)(2,1)S(1)}, bf16[512,3840]{1,0:T(8,128)(2,1)S(1)}) custom-call(s32[11]{0:T(128)S(1)} %copy-done.7, s32[10,5]{1,0:T(8,128)S(1)} %bitcast.46, f32[18,64,256]{2,1,0:T(8,128)S(1)} %get-tuple-element.207.refs_2_, f32[18,64,256]{2,1,0:T(8,128)S(1)} %collective-permute-done.3.refs_3_, ...), custom_call_target="tpu_custom_call" | custom-call | bytes 16384 | tf_op jit(solution)/shard_map/pallas_call | solution.py:87
  73.6 1.6 %shard_map.52 = (bf16[512,768]{1,0:T(8,128)(2,1)S(1)}, f32[256,512]{1,0:T(8,128)S(1)}, bf16[512,768]{1,0:T(8,128)(2,1)S(1)}, bf16[512,1536]{1,0:T(8,128)(2,1)S(1...) custom-call(s32[11]{0:T(128)S(1)} %copy-done.7, s32[10,5]{1,0:T(8,128)S(1)} %bitcast.48, ...), custom_call_target="tpu_custom_call" | custom-call | bytes 12288 | tf_op jit(solution)/shard_map/pallas_call | solution.py:87
  75.9 1.7 %collective-permute-start.14 = (f32[10,64,128]{2,1,0:T(8,128)S(1)}, f32[10,64,128]{2,1,0:T(8,128)S(1)}, u32[]{:S(2)}, u32[]{:S(2)}) collective-permute-start(f32[10,64,128]{2,1,0:T(8,128)S(1)} %get-tuple-element.167), channel_id=1, source_target_pairs={{0,8},{1,17},{2,10},{3,19},{4,12},{5,21},{6,14},{7,23},{8,0},{9,25... | collective-permute-start | bytes 983048 | tf_op jit(solution)/shard_map/ppermute | solution.py:39
  77.6 1.7 %collective-permute-start.15 = (f32[10,64,128]{2,1,0:T(8,128)S(1)}, f32[10,64,128]{2,1,0:T(8,128)S(1)}, u32[]{:S(2)}, u32[]{:S(2)}) collective-permute-start(f32[10,64,128]{2,1,0:T(8,128)S(1)} %get-tuple-element.168), channel_id=1, source_target_pairs={{0,16},{1,9},{2,18},{3,11},{4,20},{5,13},{6,22},{7,15},{8,24},{9,1... | collective-permute-start | bytes 983048 | tf_op jit(solution)/shard_map/ppermute | solution.py:39
  79.4 13.7 %shard_map.55 = (f32[4,2,64,256]{3,2,1,0:T(8,128)S(1)}, f32[2,64,256]{2,1,0:T(8,128)S(1)}, f32[4,2,64,256]{3,2,1,0:T(8,128)S(1)}, f32[2,64,256]{2,1,0:T(8,128)S(1)}) custom-call(s32[11]{0:T(128)S(1)} %copy-done.7, f32[1024,512]{1,0:T(8,128)S(1)} %get-tuple-element.144.refs_1_, bf16[1536,768]{1,0:T(8,128)(2,1)S(1)} %get-tuple-element.145.refs_2_.refs_6_, ...), custom_call_target="tpu_custom_call" | custom-call | flops 125829120 | bytes 137216 | tf_op jit(solution)/shard_map/pallas_call | solution.py:87
  93.2 1.8 %collective-permute-start.23 = (f32[5,2,64,256]{3,2,1,0:T(8,128)S(1)}, f32[5,2,64,256]{3,2,1,0:T(8,128)S(1)}, u32[]{:S(2)}, u32[]{:S(2)}) collective-permute-start(f32[5,2,64,256]{3,2,1,0:T(8,128)S(1)} %pad_maximum_fusion.2), channel_id=1, source_target_pairs={{0,16},{1,9},{2,18},{3,11},{4,20},{5,13},{6,22},{7,15},{8,24},{9,1... | collective-permute-start | bytes 1966088 | tf_op jit(solution)/shard_map/ppermute | solution.py:39
  95.0 1.5 collective-permute-start.13
  96.4 2.4 %collective-permute-done.16.refs_4_ = f32[10,64,128]{2,1,0:T(8,128)S(1)} collective-permute-done((f32[10,64,128]{2,1,0:T(8,128)S(1)}, f32[10,64,128]{2,1,0:T(8,128)S(1)}, u32[]{:S(2)}, u32[]{:S(2)}) %collective-permute-start.16) | collective-permute-done | bytes 327712 | tf_op jit(solution)/shard_map/ppermute | solution.py:39
  98.8 8.3 %shard_map.56 = (f32[5,2,64,128]{3,2,1,0:T(8,128)S(1)}, f32[5,2,64,128]{3,2,1,0:T(8,128)S(1)}, f32[5,2,64,128]{3,2,1,0:T(8,128)S(1)}, f32[5,2,64,128]{3,2,1,0:T(...) custom-call(s32[11]{0:T(128)S(1)} %copy-done.7, f32[10,64,128]{2,1,0:T(8,128)S(1)} %get-tuple-element.166.refs_1_, ...), custom_call_target="tpu_custom_call" | custom-call | flops 78643200 | bytes 158720 | tf_op jit(solution)/shard_map/pallas_call | solution.py:87
  107.9 2.2 %collective-permute-start.21 = (f32[5,2,64,128]{3,2,1,0:T(8,128)S(1)}, f32[5,2,64,128]{3,2,1,0:T(8,128)S(1)}, u32[]{:S(2)}, u32[]{:S(2)}) collective-permute-start(f32[5,2,64,128]{3,2,1,0:T(8,128)S(1)} %get-tuple-element.182), channel_id=1, source_target_pairs={{0,16},{1,9},{2,18},{3,11},{4,20},{5,13},{6,22},{7,15},{8,24},{9,1... | collective-permute-start | bytes 983048 | tf_op jit(solution)/shard_map/ppermute | solution.py:39
  111.3 10.0 %shard_map.57 = (f32[7,2,64,128]{3,2,1,0:T(8,128)S(1)}, f32[7,2,64,128]{3,2,1,0:T(8,128)S(1)}, f32[7,2,64,128]{3,2,1,0:T(8,128)S(1)}, f32[7,2,64,128]{3,2,1,0:T(...) custom-call(s32[11]{0:T(128)S(1)} %copy-done.7, f32[10,64,128]{2,1,0:T(8,128)S(1)} %get-tuple-element.161.refs_1_, ...), custom_call_target="tpu_custom_call" | custom-call | flops 78643200 | bytes 189440 | tf_op jit(solution)/shard_map/pallas_call | solution.py:87
  121.9 1.7 %collective-permute-start.18 = (f32[7,2,64,128]{3,2,1,0:T(8,128)S(1)}, f32[7,2,64,128]{3,2,1,0:T(8,128)S(1)}, u32[]{:S(2)}, u32[]{:S(2)}) collective-permute-start(f32[7,2,64,128]{3,2,1,0:T(8,128)S(1)} %get-tuple-element.178), channel_id=1, source_target_pairs={{0,16},{1,9},{2,18},{3,11},{4,20},{5,13},{6,22},{7,15},{8,24},{9,1... | collective-permute-start | bytes 1376264 | tf_op jit(solution)/shard_map/ppermute | solution.py:39
  124.9 13.3 %shard_map.60 = (f32[3,2,64,256]{3,2,1,0:T(8,128)S(1)}, f32[2,64,256]{2,1,0:T(8,128)S(1)}, f32[2,2,64,256]{3,2,1,0:T(8,128)S(1)}, f32[2,64,256]{2,1,0:T(8,128)S(...) custom-call(s32[11]{0:T(128)S(1)} %copy-done.7, f32[768,512]{1,0:T(8,128)S(1)} %copy-done.5, ...), custom_call_target="tpu_custom_call" | custom-call | flops 125829120 | bytes 92160 | tf_op jit(solution)/shard_map/pallas_call | solution.py:87
  138.3 2.3 %shard_map.58.refs_5_ = f32[1,10,5,2,64,256]{5,4,3,2,1,0:T(8,128)} custom-call(s32[11]{0:T(128)S(1)} %copy-done.7, f32[4,2,64,256]{3,2,1,0:T(8,128)S(1)} %get-tuple-element.184.refs_1_, f32[4,2,64,256]{3,2,1,0:T(8,128)S(1)} %slice.76.refs_2_), custom_call_target="tpu_custom_call" | custom-call | bytes 4096 | tf_op jit(solution)/shard_map/pallas_call | solution.py:87
  140.6 1.7 %shard_map.59.refs_5_ = f32[1,10,5,2,64,256]{5,4,3,2,1,0:T(8,128)} custom-call(s32[11]{0:T(128)S(1)} %copy-done.7, f32[5,2,64,128]{3,2,1,0:T(8,128)S(1)} %get-tuple-element.180.refs_1_, f32[5,2,64,128]{3,2,1,0:T(8,128)S(1)} %collective-permute-done.20.refs_2_, f32[5,2,64,128]{3,2,1,0:T(8,128)S(1)} %collective-permute-done.21.refs_3_, ...), custom_call_target="tpu_custom_call", output_to_operand_aliasing={{}: (5, {})} | custom-call | bytes 30720 | tf_op jit(solution)/shard_map/pallas_call | solution.py:87
  142.3 3.1 %collective-permute-done.19.refs_4_ = f32[7,2,64,128]{3,2,1,0:T(8,128)S(1)} collective-permute-done((f32[7,2,64,128]{3,2,1,0:T(8,128)S(1)}, f32[7,2,64,128]{3,2,1,0:T(8,128)S(1)}, u32[]{:S(2)}, u32[]{:S(2)}) %collective-permute-start.19) | collective-permute-done | bytes 458784 | tf_op jit(solution)/shard_map/ppermute | solution.py:39
  145.4 3.0 %shard_map.61 = (f32[1,10,5,2,64,256]{5,4,3,2,1,0:T(8,128)}, f32[1,10,2,64,256]{4,3,2,1,0:T(8,128)}) custom-call(s32[11]{0:T(128)S(1)} %copy-done.7, f32[7,2,64,128]{3,2,1,0:T(8,128)S(1)} %get-tuple-element.176.refs_1_, f32[7,2,64,128]{3,2,1,0:T(8,128)S(1)} %collective-permute-done.17.refs_2_, ...), custom_call_target="tpu_custom_call", output_to_operand_aliasing={{0}: (5, {})} | custom-call | bytes 43520 | tf_op jit(solution)/shard_map/pallas_call | solution.py:87
  (74 shorter events, 19.8 us)
Async XLA Ops:
  4.8 10.9 %copy-start.9 = (s32[1,10,5]{1,0,2:T(1,128)S(1)}, s32[1,10,5]{1,0,2:T(1,128)}, u32[]{:S(2)}) copy-start(s32[1,10,5]{1,0,2:T(1,128)} %param.5) | copy-start | bytes 604
  6.1 29.7 %collective-permute-start.4 = (f32[18,64,256]{2,1,0:T(8,128)}, f32[18,64,256]{2,1,0:T(8,128)S(1)}, u32[]{:S(2)}, u32[]{:S(2)}) collective-permute-start(f32[18,64,256]{2,1,0:T(8,128)} %get-tuple-element.206), channel_id=1, source_target_pairs={{0,16},{1,9},{2,18},{3,11},{4,20},{5,13},{6,22},{7,15},{8,24},{9,1... | collective-permute-start | bytes 3538952 | tf_op jit(solution)/shard_map/ppermute | solution.py:39
  9.1 26.8 %collective-permute-start.3 = (f32[18,64,256]{2,1,0:T(8,128)S(1)}, f32[18,64,256]{2,1,0:T(8,128)S(1)}, u32[]{:S(2)}, u32[]{:S(2)}) collective-permute-start(f32[18,64,256]{2,1,0:T(8,128)S(1)} %get-tuple-element.207.refs_2_), channel_id=1, source_target_pairs={{0,8},{1,17},{2,10},{3,19},{4,12},{5,21},{6,14},{7,23},{8,0},{9,25... | collective-permute-start | bytes 3538952 | tf_op jit(solution)/shard_map/ppermute | solution.py:39
  10.5 10.7 %collective-permute-start = (f32[2,64,256]{2,1,0:T(8,128)}, f32[2,64,256]{2,1,0:T(8,128)}, u32[]{:S(2)}, u32[]{:S(2)}) collective-permute-start(f32[2,64,256]{2,1,0:T(8,128)} %get-tuple-element.205), channel_id=1, source_target_pairs={{0,4},{8,12},{16,20},{24,28}} | collective-permute-start | bytes 393224 | tf_op jit(solution)/shard_map/ppermute | solution.py:540
  20.3 6.8 %copy-start.6 = (s32[1,10,5]{2,1,0:T(8,128)S(1)}, s32[1,10,5]{2,1,0:T(8,128)}, u32[]{:S(2)}) copy-start(s32[1,10,5]{2,1,0:T(8,128)} %copy.23) | copy-start | bytes 604
  20.3 6.8 %copy-start.7 = (s32[11]{0:T(128)S(1)}, s32[11]{0:T(128)}, u32[]{:S(2)}) copy-start(s32[11]{0:T(128)} %stack.54.refs_0_) | copy-start | bytes 136
  23.0 8.0 %collective-permute-start.2 = (f32[6,64,256]{2,1,0:T(8,128)}, f32[6,64,256]{2,1,0:T(8,128)}, u32[]{:S(2)}, u32[]{:S(2)}) collective-permute-start(f32[6,64,256]{2,1,0:T(8,128)} %pad_maximum_fusion.5), channel_id=1, source_target_pairs={{0,3},{4,7},{8,11},{12,15},{16,19},{20,23},{24,27},{28,31}} | collective-permute-start | bytes 1179656 | tf_op jit(solution)/shard_map/ppermute | solution.py:549
  25.0 6.0 %collective-permute-start.1 = (f32[6,64,256]{2,1,0:T(8,128)}, f32[6,64,256]{2,1,0:T(8,128)}, u32[]{:S(2)}, u32[]{:S(2)}) collective-permute-start(f32[6,64,256]{2,1,0:T(8,128)} %pad_maximum_fusion.5), channel_id=1, source_target_pairs={{0,1},{4,5},{8,9},{12,13},{16,17},{20,21},{24,25},{28,29}} | collective-permute-start | bytes 1179656 | tf_op jit(solution)/shard_map/ppermute | solution.py:546
  31.0 4.9 %copy-start.8 = (f32[6,64,256]{2,1,0:T(8,128)S(1)}, f32[6,64,256]{2,1,0:T(8,128)}, u32[]{:S(2)}) copy-start(f32[6,64,256]{2,1,0:T(8,128)} %get-tuple-element.103) | copy-start | bytes 1179652
  37.3 4.4 %slice-start = ((f32[18,64,256]{2,1,0:T(8,128)}), f32[8,64,256]{2,1,0:T(8,128)S(1)}, s32[]{:S(2)}) async-start(f32[18,64,256]{2,1,0:T(8,128)} %copy-done.1), calls=%async_computation | async-start | bytes 1048576 | tf_op jit(solution)/shard_map/slice | solution.py:581
  37.3 11.5 %collective-permute-start.6 = (f32[6,64,256]{2,1,0:T(8,128)S(1)}, f32[6,64,256]{2,1,0:T(8,128)S(1)}, u32[]{:S(2)}, u32[]{:S(2)}) collective-permute-start(f32[6,64,256]{2,1,0:T(8,128)S(1)} %get-tuple-element.199), channel_id=1, source_target_pairs={{0,8},{1,17},{2,10},{3,19},{4,12},{5,21},{6,14},{7,23},{8,0},{9,25... | collective-permute-start | bytes 1179656 | tf_op jit(solution)/shard_map/ppermute | solution.py:39
  38.4 12.1 %collective-permute-start.5 = (f32[6,64,256]{2,1,0:T(8,128)S(1)}, f32[6,64,256]{2,1,0:T(8,128)S(1)}, u32[]{:S(2)}, u32[]{:S(2)}) collective-permute-start(f32[6,64,256]{2,1,0:T(8,128)S(1)} %get-tuple-element.199), channel_id=1, source_target_pairs={{0,16},{1,9},{2,18},{3,11},{4,20},{5,13},{6,22},{7,15},{8,24},{9,1... | collective-permute-start | bytes 1179656 | tf_op jit(solution)/shard_map/ppermute | solution.py:39
  40.1 16.3 %collective-permute-start.7 = (f32[10,64,256]{2,1,0:T(8,128)S(1)}, f32[10,64,256]{2,1,0:T(8,128)S(1)}, u32[]{:S(2)}, u32[]{:S(2)}) collective-permute-start(f32[10,64,256]{2,1,0:T(8,128)S(1)} %slice.67), channel_id=1, source_target_pairs={{0,8},{1,17},{2,10},{3,19},{4,12},{5,21},{6,14},{7,23},{8,0},{9,25... | collective-permute-start | bytes 1966088 | tf_op jit(solution)/shard_map/ppermute | solution.py:39
  50.5 19.1 %copy-start.2 = (f32[18,64,256]{2,1,0:T(8,128)S(1)}, f32[18,64,256]{2,1,0:T(8,128)}, u32[]{:S(2)}) copy-start(f32[18,64,256]{2,1,0:T(8,128)} %copy-done.1) | copy-start | bytes 3538948
  56.4 13.1 %collective-permute-start.8 = (f32[7,64,256]{2,1,0:T(8,128)S(1)}, f32[7,64,256]{2,1,0:T(8,128)S(1)}, u32[]{:S(2)}, u32[]{:S(2)}) collective-permute-start(f32[7,64,256]{2,1,0:T(8,128)S(1)} %get-tuple-element.114), channel_id=1, source_target_pairs={{0,8},{1,17},{2,10},{3,19},{4,12},{5,21},{6,14},{7,23},{8,0},{9,25... | collective-permute-start | bytes 1376264 | tf_op jit(solution)/shard_map/ppermute | solution.py:39
  57.3 12.3 %collective-permute-start.9 = (f32[7,64,256]{2,1,0:T(8,128)S(1)}, f32[7,64,256]{2,1,0:T(8,128)S(1)}, u32[]{:S(2)}, u32[]{:S(2)}) collective-permute-start(f32[7,64,256]{2,1,0:T(8,128)S(1)} %get-tuple-element.115), channel_id=1, source_target_pairs={{0,16},{1,9},{2,18},{3,11},{4,20},{5,13},{6,22},{7,15},{8,24},{9,1... | collective-permute-start | bytes 1376264 | tf_op jit(solution)/shard_map/ppermute | solution.py:39
  69.6 4.1 %collective-permute-start.10 = (f32[24,64,256]{2,1,0:T(8,128)S(1)}, f32[24,64,256]{2,1,0:T(8,128)S(1)}, u32[]{:S(2)}, u32[]{:S(2)}) collective-permute-start(f32[24,64,256]{2,1,0:T(8,128)S(1)} %slice_dynamic-update-slice_fusion.refs_2_), channel_id=1, source_target_pairs={{0,1},{1,0},{2,3},{3,2},{4,5},{5,4},{6,7},{7,6},{8,9},{9,8},{10,11... | collective-permute-start | bytes 4718600 | tf_op jit(solution)/shard_map/ppermute | solution.py:29
  75.3 17.8 %collective-permute-start.11 = (f32[10,64,128]{2,1,0:T(8,128)S(1)}, f32[10,64,128]{2,1,0:T(8,128)S(1)}, u32[]{:S(2)}, u32[]{:S(2)}) collective-permute-start(f32[10,64,128]{2,1,0:T(8,128)S(1)} %get-tuple-element.158), channel_id=1, source_target_pairs={{0,8},{1,17},{2,10},{3,19},{4,12},{5,21},{6,14},{7,23},{8,0},{9,25... | collective-permute-start | bytes 983048 | tf_op jit(solution)/shard_map/ppermute | solution.py:39
  75.6 17.5 %collective-permute-start.12 = (f32[10,64,128]{2,1,0:T(8,128)S(1)}, f32[10,64,128]{2,1,0:T(8,128)S(1)}, u32[]{:S(2)}, u32[]{:S(2)}) collective-permute-start(f32[10,64,128]{2,1,0:T(8,128)S(1)} %get-tuple-element.159), channel_id=1, source_target_pairs={{0,16},{1,9},{2,18},{3,11},{4,20},{5,13},{6,22},{7,15},{8,24},{9,1... | collective-permute-start | bytes 983048 | tf_op jit(solution)/shard_map/ppermute | solution.py:39
  75.9 20.5 %collective-permute-start.14 = (f32[10,64,128]{2,1,0:T(8,128)S(1)}, f32[10,64,128]{2,1,0:T(8,128)S(1)}, u32[]{:S(2)}, u32[]{:S(2)}) collective-permute-start(f32[10,64,128]{2,1,0:T(8,128)S(1)} %get-tuple-element.167), channel_id=1, source_target_pairs={{0,8},{1,17},{2,10},{3,19},{4,12},{5,21},{6,14},{7,23},{8,0},{9,25... | collective-permute-start | bytes 983048 | tf_op jit(solution)/shard_map/ppermute | solution.py:39
  77.6 18.8 %collective-permute-start.15 = (f32[10,64,128]{2,1,0:T(8,128)S(1)}, f32[10,64,128]{2,1,0:T(8,128)S(1)}, u32[]{:S(2)}, u32[]{:S(2)}) collective-permute-start(f32[10,64,128]{2,1,0:T(8,128)S(1)} %get-tuple-element.168), channel_id=1, source_target_pairs={{0,16},{1,9},{2,18},{3,11},{4,20},{5,13},{6,22},{7,15},{8,24},{9,1... | collective-permute-start | bytes 983048 | tf_op jit(solution)/shard_map/ppermute | solution.py:39
  79.4 19.4 %collective-permute-start.16 = (f32[10,64,128]{2,1,0:T(8,128)S(1)}, f32[10,64,128]{2,1,0:T(8,128)S(1)}, u32[]{:S(2)}, u32[]{:S(2)}) collective-permute-start(f32[10,64,128]{2,1,0:T(8,128)S(1)} %get-tuple-element.169), channel_id=1, source_target_pairs={{0,24},{1,25},{2,26},{3,27},{4,28},{5,29},{6,30},{7,31},{8,16},{9,... | collective-permute-start | bytes 983048 | tf_op jit(solution)/shard_map/ppermute | solution.py:39
  93.2 30.4 %collective-permute-start.23 = (f32[5,2,64,256]{3,2,1,0:T(8,128)S(1)}, f32[5,2,64,256]{3,2,1,0:T(8,128)S(1)}, u32[]{:S(2)}, u32[]{:S(2)}) collective-permute-start(f32[5,2,64,256]{3,2,1,0:T(8,128)S(1)} %pad_maximum_fusion.2), channel_id=1, source_target_pairs={{0,16},{1,9},{2,18},{3,11},{4,20},{5,13},{6,22},{7,15},{8,24},{9,1... | collective-permute-start | bytes 1966088 | tf_op jit(solution)/shard_map/ppermute | solution.py:39
  95.0 16.3 %collective-permute-start.13 = (f32[10,64,128]{2,1,0:T(8,128)S(1)}, f32[10,64,128]{2,1,0:T(8,128)S(1)}, u32[]{:S(2)}, u32[]{:S(2)}) collective-permute-start(f32[10,64,128]{2,1,0:T(8,128)S(1)} %get-tuple-element.164), channel_id=1, source_target_pairs={{0,24},{1,25},{2,26},{3,27},{4,28},{5,29},{6,30},{7,31},{8,16},{9,... | collective-permute-start | bytes 983048 | tf_op jit(solution)/shard_map/ppermute | solution.py:39
  107.2 14.7 %collective-permute-start.20 = (f32[5,2,64,128]{3,2,1,0:T(8,128)S(1)}, f32[5,2,64,128]{3,2,1,0:T(8,128)S(1)}, u32[]{:S(2)}, u32[]{:S(2)}) collective-permute-start(f32[5,2,64,128]{3,2,1,0:T(8,128)S(1)} %get-tuple-element.181), channel_id=1, source_target_pairs={{0,8},{1,17},{2,10},{3,19},{4,12},{5,21},{6,14},{7,23},{8,0},{9,25... | collective-permute-start | bytes 983048 | tf_op jit(solution)/shard_map/ppermute | solution.py:39
  107.9 32.7 %collective-permute-start.21 = (f32[5,2,64,128]{3,2,1,0:T(8,128)S(1)}, f32[5,2,64,128]{3,2,1,0:T(8,128)S(1)}, u32[]{:S(2)}, u32[]{:S(2)}) collective-permute-start(f32[5,2,64,128]{3,2,1,0:T(8,128)S(1)} %get-tuple-element.182), channel_id=1, source_target_pairs={{0,16},{1,9},{2,18},{3,11},{4,20},{5,13},{6,22},{7,15},{8,24},{9,1... | collective-permute-start | bytes 983048 | tf_op jit(solution)/shard_map/ppermute | solution.py:39
  110.0 30.6 %collective-permute-start.22 = (f32[5,2,64,128]{3,2,1,0:T(8,128)S(1)}, f32[5,2,64,128]{3,2,1,0:T(8,128)S(1)}, u32[]{:S(2)}, u32[]{:S(2)}) collective-permute-start(f32[5,2,64,128]{3,2,1,0:T(8,128)S(1)} %get-tuple-element.183), channel_id=1, source_target_pairs={{0,24},{1,25},{2,26},{3,27},{4,28},{5,29},{6,30},{7,31},{8,16},{9,... | collective-permute-start | bytes 983048 | tf_op jit(solution)/shard_map/ppermute | solution.py:39
  111.2 13.6 %copy-start.5 = (f32[768,512]{1,0:T(8,128)S(1)}, f32[768,512]{1,0:T(8,128)}, u32[]{:S(2)}) copy-start(f32[768,512]{1,0:T(8,128)} %copy-done.4) | copy-start | bytes 4718596
  121.3 21.0 %collective-permute-start.17 = (f32[7,2,64,128]{3,2,1,0:T(8,128)S(1)}, f32[7,2,64,128]{3,2,1,0:T(8,128)S(1)}, u32[]{:S(2)}, u32[]{:S(2)}) collective-permute-start(f32[7,2,64,128]{3,2,1,0:T(8,128)S(1)} %get-tuple-element.177), channel_id=1, source_target_pairs={{0,8},{1,17},{2,10},{3,19},{4,12},{5,21},{6,14},{7,23},{8,0},{9,25... | collective-permute-start | bytes 1376264 | tf_op jit(solution)/shard_map/ppermute | solution.py:39
  121.9 20.4 %collective-permute-start.18 = (f32[7,2,64,128]{3,2,1,0:T(8,128)S(1)}, f32[7,2,64,128]{3,2,1,0:T(8,128)S(1)}, u32[]{:S(2)}, u32[]{:S(2)}) collective-permute-start(f32[7,2,64,128]{3,2,1,0:T(8,128)S(1)} %get-tuple-element.178), channel_id=1, source_target_pairs={{0,16},{1,9},{2,18},{3,11},{4,20},{5,13},{6,22},{7,15},{8,24},{9,1... | collective-permute-start | bytes 1376264 | tf_op jit(solution)/shard_map/ppermute | solution.py:39
  123.6 21.8 %collective-permute-start.19 = (f32[7,2,64,128]{3,2,1,0:T(8,128)S(1)}, f32[7,2,64,128]{3,2,1,0:T(8,128)S(1)}, u32[]{:S(2)}, u32[]{:S(2)}) collective-permute-start(f32[7,2,64,128]{3,2,1,0:T(8,128)S(1)} %get-tuple-element.179), channel_id=1, source_target_pairs={{0,24},{1,25},{2,26},{3,27},{4,28},{5,29},{6,30},{7,31},{8,16},{9,... | collective-permute-start | bytes 1376264 | tf_op jit(solution)/shard_map/ppermute | solution.py:39
  140.6 4.8 %copy-start.3 = (f32[1,10,2,64,256]{4,3,2,1,0:T(8,128)S(1)}, f32[1,10,2,64,256]{4,3,2,1,0:T(8,128)}, u32[]{:S(2)}) copy-start(f32[1,10,2,64,256]{4,3,2,1,0:T(8,128)} %refs_6_.1) | copy-start | bytes 3932164
  (3 other events, 5.5 us)
